TPU v7x, 128 devices: a whole 4x4x4 slice. The times are simulated.
128 devices in a mesh: wide: 32 (over x, z, core), narrow: 4 (over y).
Axes of the slice: x: 4, y: 4, z: 4, core: 2. Of those that a mesh axis runs over, the one named last changes fastest.
Arguments:
- deltas: bfloat16 [32, 4718592], P('wide', 'narrow'), may hold values from -64 to 64
- sample_counts: int32 [32], replicated, may hold values from 200 to 4999
- momentum: float32 [4718592], P('narrow'), may hold values from -3 to 3
- weights: float32 [4718592], P('narrow'), may hold values from -6 to 6
Outputs:
- new_weights: float32 [4718592], P('narrow')
- new_momentum: float32 [4718592], P('narrow')
All inputs are finite; a program needn't handle non-finite values.
Results may differ from a plain program's by a relative error of at most 0.0003.
Values may be sent and summed in bfloat16 or wider, within the bound.
No kernel may reach another device: no remote copies, remote signals or barrier semaphores. Data moves between devices by JAX's collectives and lax.ppermute only.
A program may use at most 128 MiB of HBM per device.

v0:
```python
import jax
import jax.numpy as jnp
from jax import lax
from jax.sharding import PartitionSpec as P

ITERS = 3


NU_SQUARE = 1.0
MOMENTUM_RATE = 0.9
SERVER_RATE = 1.0


def shards(deltas, sample_counts, momentum, weights):
    counts = sample_counts.astype(jnp.float32)
    client_share = counts / jnp.sum(counts)
    regrouped = lax.all_to_all(deltas, "wide", split_axis=1, concat_axis=0, tiled=True)

    def weighted(coefficients):
        return jnp.sum(coefficients[:, None] * regrouped.astype(jnp.float32), axis=0)

    median = weighted(client_share)
    for sweep in range(ITERS):
        partial_sums = jnp.sum(jnp.square(regrouped.astype(jnp.float32) - median[None, :]), axis=1)
        squared = lax.psum(partial_sums, ("wide", "narrow"))
        beta_weights = client_share / jnp.sqrt(squared + NU_SQUARE)
        median = weighted(beta_weights) / jnp.sum(beta_weights)
    gathered = lax.all_gather(median, "wide", axis=0, tiled=True)
    new_momentum = MOMENTUM_RATE * momentum + gathered
    new_weights = weights + SERVER_RATE * new_momentum
    return (new_weights, new_momentum)


def solution(mesh):
    placed = (P("wide", "narrow"), P(), P("narrow"), P("narrow"))
    return jax.shard_map(
        shards, mesh=mesh, in_specs=placed, out_specs=(P("narrow"), P("narrow")), check_vma=False
    )
```

profile of v0, /device:TPU:1, one launch (start us, length us, event | category | flops | bytes accessed | tf_op | source)
XLA Modules:
  0.0 375.9 jit_solution(16055560878746382559)
XLA Ops:
  7.2 0.5 broadcast.23
  7.7 15.5 %reduce = bf16[32,36864]{1,0:T(8,128)(2,1)S(1)} reduce(bf16[32,1,36864]{2,1,0:T(2,128)(2,1)} %bitcast.32, bf16[]{:T(256)} %broadcast.23), dimensions={1}, to_apply=%bitcast.29.reduce_sub_computation | reduce | bytes 4718594
  23.1 0.0 copy-start.2
  23.2 3.0 reshape.24
  26.2 9.4 %all-to-all-start = ((bf16[32,2,18432]{2,1,0:T(2,128)(2,1)}), bf16[32,2,18432]{2,1,0:T(2,128)(2,1)S(1)}, u32[]{:S(2)}, u32[]{:S(2)}) async-start(bf16[32,2,18432]{2,1,0:T(2,128)(2,1)} %reshape.24), calls=%async_computation | async-start | bytes 4718592 | tf_op jit(solution)/shard_map/all_to_all | solution.py:17
  35.6 0.2 all-gather.2.cloned.1.call-start
  35.8 0.0 copy-done.2
  35.8 0.7 convert_reduce_fusion
  36.5 0.7 convert_divide_fusion
  37.2 29.5 %all-to-all-done = bf16[32,2,18432]{2,1,0:T(2,128)(2,1)S(1)} async-done(((bf16[32,2,18432]{2,1,0:T(2,128)(2,1)}), bf16[32,2,18432]{2,1,0:T(2,128)(2,1)S(1)}, u32[]{:S(2)}, u32[]{:S(2)}) %all-to-all-start) | async-done | bytes 2359328 | tf_op jit(solution)/shard_map/all_to_all | solution.py:17
  66.7 6.9 %reshape.25 = bf16[32,1,36864]{2,1,0:T(2,128)(2,1)} reshape(bf16[32,2,18432]{2,1,0:T(2,128)(2,1)S(1)} %all-to-all-done) | data formatting | bytes 4718592
  73.7 9.4 %bitcast_convert_fusion = f32[1,32,36864]{2,0,1:T(1,128)} fusion(bf16[32,1,36864]{2,1,0:T(2,128)(2,1)} %reshape.25), kind=kLoop, calls=%fused_computation.30 | loop fusion | flops 1179648 | bytes 7077888 | tf_op jit(solution)/shard_map/convert_element_type | solution.py:24
  83.0 6.0 %fusion = f32[36864]{0:T(1024)S(1)} fusion(f32[1,32,36864]{2,0,1:T(1,128)} %bitcast_convert_fusion, f32[32]{0:T(128)S(1)} %convert_divide_fusion), kind=kLoop, calls=%fused_computation.7 | loop fusion | flops 2322432 | bytes 4866176 | tf_op jit(solution)/shard_map/reduce_sum | solution.py:20
  89.1 0.0 copy-done
  89.1 2.6 fusion.2
  91.7 65.0 %psum.21 = f32[32]{0:T(128)S(1)} all-reduce(f32[32]{0:T(128)S(1)} %fusion.2), channel_id=1, replica_groups=mesh['wide'=32,'narrow'=4] {'wide','narrow'}, use_global_device_ids=true, to_apply=%region_3.0 | all-reduce | flops 32 | bytes 256 | tf_op jit(solution)/shard_map/psum | solution.py:25
  156.7 1.4 fusion.13
  158.1 5.9 %fusion.3 = f32[36864]{0:T(1024)S(1)} fusion(f32[1,32,36864]{2,0,1:T(1,128)} %bitcast_convert_fusion, f32[32]{0:T(128)S(1)} %get-tuple-element.9), kind=kLoop, calls=%fused_computation.10 | loop fusion | flops 2322432 | bytes 4866176 | tf_op jit(solution)/shard_map/reduce_sum | solution.py:20
  164.0 0.7 broadcast_divide_fusion.2
  164.7 2.6 fusion.5
  167.3 62.9 %psum.22 = f32[32]{0:T(128)S(1)} all-reduce(f32[32]{0:T(128)S(1)} %fusion.5), channel_id=1, replica_groups=mesh['wide'=32,'narrow'=4] {'wide','narrow'}, use_global_device_ids=true, to_apply=%region_7.0 | all-reduce | flops 32 | bytes 256 | tf_op jit(solution)/shard_map/psum | solution.py:25
  230.2 1.3 fusion.12
  231.5 5.9 %fusion.6 = f32[36864]{0:T(1024)S(1)} fusion(f32[1,32,36864]{2,0,1:T(1,128)} %bitcast_convert_fusion, f32[32]{0:T(128)S(1)} %get-tuple-element.7), kind=kLoop, calls=%fused_computation.13 | loop fusion | flops 2322432 | bytes 4866176 | tf_op jit(solution)/shard_map/reduce_sum | solution.py:20
  237.4 0.7 broadcast_divide_fusion.1
  238.1 5.0 %fusion.8 = f32[32]{0:T(128)S(1)} fusion(f32[1,32,36864]{2,0,1:T(1,128)} %bitcast_convert_fusion, f32[36864]{0:T(1024)S(1)} %broadcast_divide_fusion.1), kind=kLoop, calls=%fused_computation.15 | loop fusion | flops 3538912 | bytes 4866176 | tf_op jit(solution)/shard_map/reduce_sum | solution.py:24
  243.0 64.4 %psum.23 = f32[32]{0:T(128)S(1)} all-reduce(f32[32]{0:T(128)S(1)} %fusion.8), channel_id=1, replica_groups=mesh['wide'=32,'narrow'=4] {'wide','narrow'}, use_global_device_ids=true, to_apply=%region_11.0 | all-reduce | flops 32 | bytes 256 | tf_op jit(solution)/shard_map/psum | solution.py:25
  307.4 1.3 fusion.11
  308.7 5.9 %fusion.9 = f32[36864]{0:T(1024)S(1)} fusion(f32[1,32,36864]{2,0,1:T(1,128)} %bitcast_convert_fusion, f32[32]{0:T(128)S(1)} %get-tuple-element.5), kind=kLoop, calls=%fused_computation.16 | loop fusion | flops 2322432 | bytes 4866176 | tf_op jit(solution)/shard_map/reduce_sum | solution.py:20
  314.6 1.2 broadcast_divide_fusion
  315.8 0.0 all-gather.2.cloned.1.call-update
  315.9 44.0 %all-gather.2.cloned.1.call-done = f32[1179648]{0:T(1024)} async-done(((f32[36864]{0:T(1024)}), f32[1179648]{0:T(1024)}) %all-gather.2.cloned.1.call-update) | async-done | bytes 4718608 | tf_op jit(solution)/shard_map/all_gather | solution.py:28
  359.8 9.2 %fusion.10 = (f32[1179648]{0:T(1024)}, f32[1179648]{0:T(1024)}) fusion(f32[1179648]{0:T(1024)} %param.7, f32[1179648]{0:T(1024)} %all-gather.2.cloned.1.call-done, f32[1179648]{0:T(1024)} %param.6), kind=kLoop, calls=%fused_computation.26 | loop fusion | flops 3538944 | bytes 23592960 | tf_op jit(solution)/shard_map/add | solution.py:30
  (3 shorter events, 0.0 us)
Async XLA Ops:
  23.1 12.7 %copy-start.2 = (s32[32]{0:T(128)S(1)}, s32[32]{0:T(128)}, u32[]{:S(2)}) copy-start(s32[32]{0:T(128)} %param.5) | copy-start | bytes 388
  26.2 40.6 %all-to-all-start = ((bf16[32,2,18432]{2,1,0:T(2,128)(2,1)}), bf16[32,2,18432]{2,1,0:T(2,128)(2,1)S(1)}, u32[]{:S(2)}, u32[]{:S(2)}) async-start(bf16[32,2,18432]{2,1,0:T(2,128)(2,1)} %reshape.24), calls=%async_computation | async-start | bytes 4718592 | tf_op jit(solution)/shard_map/all_to_all | solution.py:17
  35.6 324.2 %all-gather.2.cloned.1.call-start = ((), (), s32[]{:S(2)}) async-start(), calls=%async_computation.1 | async-start | bytes 4866048 | tf_op jit(solution)/shard_map/all_gather | solution.py:28
  83.0 6.0 %copy-start = (f32[1,32,36864]{2,0,1:T(1,128)S(1)}, f32[1,32,36864]{2,0,1:T(1,128)}, u32[]{:S(2)}) copy-start(f32[1,32,36864]{2,0,1:T(1,128)} %bitcast_convert_fusion) | copy-start | bytes 14155780
  156.7 8.0 %copy-start.1 = (f32[1,32,36864]{2,0,1:T(1,128)S(1)}, f32[1,32,36864]{2,0,1:T(1,128)}, u32[]{:S(2)}) copy-start(f32[1,32,36864]{2,0,1:T(1,128)} %bitcast_convert_fusion) | copy-start | bytes 14155780
Sparse Core Ops, SparseCore 0:
  316.0 43.7 all-gather.1
where the time goes:
time: 377 us; the launch traced here: 376 us
  blocking collectives  192 us (51%)
  other arithmetic  75.8 us (20%)
  waiting for transfers between devices  73.5 us (19%)
  between operations  14.1 us (4%)
  local copies, waits for them, and re-layouts  10.5 us (3%)
  starting transfers between devices  9.65 us (3%)
    psum x3, blocking collectives, shards(): squared = lax.psum(partial_sums, ('wide', 'narrow'))  192 us
    all_gather x1, waiting for transfers between devices, shards(): gathered = lax.all_gather(median, 'wide', axis=0, tiled=True)  44 us
    all_to_all x1, waiting for transfers between devices, shards(): lax.all_to_all(deltas, 'wide', split_axis=1, concat_axis=0, tiled=True)  29.5 us
    reduce_sum x4, other arithmetic, weighted(): jnp.sum(coefficients[:, None] * regrouped.astype(jnp.float32), axis=0)  23.7 us
    unnamed x1, other arithmetic  15.5 us
    unnamed x9, local copies, waits for them, and re-layouts  10.5 us
    reduce_sum x3, other arithmetic, shards(): jnp.sum(jnp.square(regrouped.astype(jnp.float32) - median[None, :]), axis=1)  10.2 us
    all_to_all x1, starting transfers between devices, shards(): lax.all_to_all(deltas, 'wide', split_axis=1, concat_axis=0, tiled=True)  9.43 us
  transfers between devices with their start and end apart: 2, of which 2 were waited for; matrix products, arithmetic and copies ran while one was open for 0% of the time, Pallas kernels for 0%

commit v1 on v0

v1 whole, which is shorter than its diff:
```python
import jax
import jax.numpy as jnp
from jax import lax
from jax.experimental import pallas as pl
from jax.experimental.pallas import tpu as pltpu
from jax.sharding import PartitionSpec as P

ITERS = 3


NU_SQUARE = 1.0
MOMENTUM_RATE = 0.9
SERVER_RATE = 1.0

LANES = 128
GROUP = 16
SENT_TOP = 16376.0
SMALLEST_NORM = 1e-17
SAFE_SHARE = 1.0 / 256.0
VMEM = 48 << 20


def pack_kernel(flat_ref, packed_ref):
    packed_ref[...] = flat_ref[...].reshape(packed_ref.shape)


def pack(deltas, clients):
    entries = deltas.shape[1]
    rows = entries // LANES
    steps = 2
    packed = pl.pallas_call(
        pack_kernel,
        grid=(steps,),
        in_specs=[pl.BlockSpec((1, entries // steps), lambda i: (0, i))],
        out_specs=pl.BlockSpec((rows // steps, LANES), lambda i: (i, 0)),
        out_shape=jax.ShapeDtypeStruct((rows, LANES), deltas.dtype),
        compiler_params=pltpu.CompilerParams(vmem_limit_bytes=VMEM),
    )(deltas)
    return packed.reshape(clients, rows // clients, LANES)


def gram_kernel(x_ref, out_ref):
    clients, rows, _ = x_ref.shape
    wide = clients * GROUP
    y = jnp.concatenate(
        [x_ref[:, pl.ds(GROUP * k, GROUP), :].reshape(wide, LANES) for k in range(rows // GROUP)], axis=1
    )
    products = lax.dot_general(y, y, (((1,), (1,)), ((), ())), preferred_element_type=jnp.float32)
    row = lax.broadcasted_iota(jnp.int32, products.shape, 0)
    column = lax.broadcasted_iota(jnp.int32, products.shape, 1)
    products = jnp.where((row & (GROUP - 1)) == (column & (GROUP - 1)), products, 0.0)
    summed = products.reshape(clients, GROUP, wide).sum(axis=1)
    owner = lax.broadcasted_iota(jnp.int32, (wide, LANES), 0) // GROUP
    lane = lax.broadcasted_iota(jnp.int32, (wide, LANES), 1)
    gram = jnp.zeros((8, LANES), jnp.float32)
    for b in range(clients // 8):
        place = jnp.where(lane == owner + clients * b, 1.0, 0.0)
        gram = gram + jnp.dot(
            summed[8 * b : 8 * b + 8], place, precision=lax.Precision.HIGHEST, preferred_element_type=jnp.float32
        )
    out_ref[...] = jnp.broadcast_to(gram[None], out_ref.shape)


def gram_copies(x, copies):
    return pl.pallas_call(
        gram_kernel,
        out_shape=jax.ShapeDtypeStruct((copies, 8, LANES), jnp.float32),
        compiler_params=pltpu.CompilerParams(vmem_limit_bytes=VMEM),
    )(x)


def median_kernel(grams_ref, counts_ref, x_ref, median_ref, facts_ref, beta_ref):
    clients, rows, _ = x_ref.shape
    packed = jnp.sum(grams_ref[...], axis=0)
    lane = lax.broadcasted_iota(jnp.int32, (clients, LANES), 1)
    row = lax.broadcasted_iota(jnp.int32, (clients, LANES), 0)
    gram = jnp.concatenate(
        [packed] + [pltpu.roll(packed, LANES - clients * b, 1) for b in range(1, clients // 8)], axis=0
    )
    gram = jnp.where(lane < clients, gram, 0.0)
    square = jnp.where(lane == row, gram, 0.0).sum(axis=0, keepdims=True)
    norm = jnp.sqrt(square)

    def as_column(values):
        return jnp.where(lane == row, values, 0.0).sum(axis=1, keepdims=True)

    counts = counts_ref[...]
    share = counts / counts.sum(axis=1, keepdims=True)
    beta = share
    safe = jnp.ones((1, 1), jnp.float32)
    for sweep in range(ITERS):
        column = as_column(beta)
        inner = (gram * column).sum(axis=0, keepdims=True)
        median_square = (inner * beta).sum(axis=1, keepdims=True)
        mean_norm = (norm * beta).sum(axis=1, keepdims=True)
        distance = square - 2.0 * inner + median_square + NU_SQUARE
        scale = norm + mean_norm
        margin = jnp.where(lane[:1] < clients, distance - SAFE_SHARE * (scale * scale), 1.0)
        safe = jnp.minimum(safe, margin.min(axis=1, keepdims=True))
        beta = share / jnp.sqrt(jnp.maximum(distance, NU_SQUARE))
        beta = beta / beta.sum(axis=1, keepdims=True)
    largest = jnp.maximum((norm * beta).sum(axis=1, keepdims=True), SMALLEST_NORM)
    up = SENT_TOP / largest
    fact = lax.broadcasted_iota(jnp.int32, facts_ref.shape, 0)
    facts_ref[...] = jnp.where(fact == 0, safe, largest * (1.0 / SENT_TOP))
    beta_ref[...] = jnp.broadcast_to(as_column(beta) * up, beta_ref.shape)
    block = 48

    def step(k, carry):
        at = pl.ds(pl.multiple_of(k * block, block), block)
        total = jnp.zeros((block, LANES), jnp.float32)
        for c in range(clients):
            total = total + beta_ref[c : c + 1, :] * x_ref[c, at, :].astype(jnp.float32)
        median_ref[at, :] = total
        return carry

    lax.fori_loop(0, rows // block, step, 0)


def median_of(grams, counts, x):
    clients, rows, _ = x.shape
    return pl.pallas_call(
        median_kernel,
        out_shape=(
            jax.ShapeDtypeStruct((rows, LANES), jnp.float32),
            jax.ShapeDtypeStruct((8, LANES), jnp.float32),
        ),
        scratch_shapes=[pltpu.VMEM((clients, LANES), jnp.float32)],
        compiler_params=pltpu.CompilerParams(vmem_limit_bytes=VMEM),
    )(grams, counts, x)


def direct(x, counts):
    share = counts / jnp.sum(counts)
    wide = x.astype(jnp.float32)

    def weighted(coefficients):
        return jnp.sum(coefficients[:, None, None] * wide, axis=0)

    median = weighted(share)
    for sweep in range(ITERS):
        squared = lax.psum(jnp.sum(jnp.square(wide - median[None]), axis=(1, 2)), ("wide", "narrow"))
        beta = share / jnp.sqrt(squared + NU_SQUARE)
        beta = beta / jnp.sum(beta)
        median = weighted(beta)
    norm = jnp.sqrt(lax.psum(jnp.sum(jnp.square(wide), axis=(1, 2)), ("wide", "narrow")))
    largest = jnp.maximum(jnp.sum(norm * beta), SMALLEST_NORM)
    return median * (SENT_TOP / largest), largest * (1.0 / SENT_TOP)


def shards(deltas, sample_counts, momentum, weights):
    clients = sample_counts.shape[0]
    counts = sample_counts.astype(jnp.float32)
    padded = jnp.pad(counts, (0, LANES - clients)).reshape(1, LANES)
    x = lax.all_to_all(pack(deltas, clients), "wide", split_axis=0, concat_axis=0, tiled=True)
    devices = lax.axis_size(("wide", "narrow"))
    grams = lax.all_to_all(gram_copies(x, devices), ("wide", "narrow"), split_axis=0, concat_axis=0, tiled=True)
    median, facts = median_of(grams, padded, x)
    median, down = lax.cond(facts[0, 0] > 0.0, lambda: (median, facts[1, 0]), lambda: direct(x, counts))
    sent = median.reshape(-1).astype(jnp.float16)
    gathered = lax.all_gather(sent, "wide", axis=0, tiled=True)
    new_momentum = MOMENTUM_RATE * momentum + gathered.astype(jnp.float32) * down
    new_weights = weights + SERVER_RATE * new_momentum
    return (new_weights, new_momentum)


def solution(mesh):
    placed = (P("wide", "narrow"), P(), P("narrow"), P("narrow"))
    return jax.shard_map(
        shards, mesh=mesh, in_specs=placed, out_specs=(P("narrow"), P("narrow")), check_vma=False
    )
```

time: 377 us -> 102 us (0.27)
  blocking collectives: 192 us -> 65.1 us
  other arithmetic: 75.8 us -> 6.49 us
  waiting for transfers between devices: 73.5 us -> 14.1 us
  between operations: 14.1 us -> 1.35 us
  local copies, waits for them, and re-layouts: 10.5 us -> 1.12 us
  Pallas kernels: 0 us -> 7.04 us
  starting transfers between devices: 9.65 us -> 5.74 us
    psum x3 -> x0, blocking collectives: 192 us -> none  [shards(): squared = lax.psum(partial_sums, ('wide', 'narrow'))]
    all_gather x1 -> x0, waiting for transfers between devices: 44 us -> none  [shards(): gathered = lax.all_gather(median, 'wide', axis=0, tiled=True)]
    all_to_all x0 -> x1, blocking collectives: none -> 40.7 us  [shards(): lax.all_to_all(pack(deltas, clients), 'wide', split_axis=0, concat_axis=0...]
    reduce_sum x11 -> x0, other arithmetic: 38.5 us -> none  [the longest x4 23.7 us: weighted(): jnp.sum(coefficients[:, None] * regrouped.astype(jnp.float32), axis=0)]
    all_gather x0 -> x1, blocking collectives: none -> 24.4 us  [shards(): gathered = lax.all_gather(sent, 'wide', axis=0, tiled=True)]
    unnamed x1 -> x0, other arithmetic: 15.5 us -> none
    all_to_all x1, waiting for transfers between devices: 29.5 us -> 14.1 us  [shards(): lax.all_to_all(gram_copies(x, devices), ('wide', 'narrow'), split_axis=0,...]
    unnamed x9 -> x2, local copies, waits for them, and re-layouts: 10.5 us -> 0.01 us
  transfers between devices with their start and end apart: 2 -> 1, of which waited for: 2 -> 1; matrix products, arithmetic and copies ran while one was open for 0% -> 0% of each run, Pallas kernels for 0% -> 0%
where the time goes in v1:
time: 102 us
  blocking collectives  65.1 us (64%)
  waiting for transfers between devices  14.1 us (14%)
  Pallas kernels  7.04 us (7%)
  other arithmetic  6.49 us (6%)
  starting transfers between devices  5.74 us (6%)
  between operations  1.35 us (1%)
  local copies, waits for them, and re-layouts  1.12 us (1%)
    all_to_all x1, blocking collectives, shards(): lax.all_to_all(pack(deltas, clients), 'wide', split_axis=0, concat_axis=0...  40.7 us
    all_gather x1, blocking collectives, shards(): gathered = lax.all_gather(sent, 'wide', axis=0, tiled=True)  24.4 us
    all_to_all x1, waiting for transfers between devices, shards(): lax.all_to_all(gram_copies(x, devices), ('wide', 'narrow'), split_axis=0,...  14.1 us
    add x1, other arithmetic, shards(): new_weights = weights + SERVER_RATE * new_momentum  6.47 us
    all_to_all x1, starting transfers between devices, shards(): lax.all_to_all(gram_copies(x, devices), ('wide', 'narrow'), split_axis=0,...  5.74 us
    pallas_call x1, Pallas kernels, gram_copies(): pl.pallas_call(gram_kernel, out_shape=jax.ShapeDtypeStruct((copies, 8, LA...  2.9 us
    pallas_call x1, Pallas kernels, pack(): pl.pallas_call(pack_kernel, grid=(steps,), in_specs=[pl.BlockSpec((1, ent...  2.56 us
  transfers between devices with their start and end apart: 1, of which 1 were waited for; matrix products, arithmetic and copies ran while one was open for 0% of the time, Pallas kernels for 0%

profile of v1, /device:TPU:1, one launch (start us, length us, event | category | flops | bytes accessed | tf_op | source)
XLA Modules:
  0.0 101.6 jit_solution(2556438220487961278)
XLA Ops:
  0.6 2.6 %shard_map.59 = bf16[9216,128]{1,0:T(8,128)(2,1)S(1)} custom-call(bf16[1,1179648]{1,0:T(2,128)(2,1)} %flat_ref.1), custom_call_target="tpu_custom_call" | custom-call | tf_op jit(solution)/shard_map/pallas_call | solution.py:31
  3.2 0.0 copy-start
  3.2 40.7 %all_to_all.10.x_ref = bf16[32,288,128]{2,1,0:T(8,128)(2,1)S(1)} all-to-all(bf16[32,288,128]{2,1,0:T(8,128)(2,1)S(1)} %bitcast.7), channel_id=1, replica_groups=mesh['wide'=32,'narrow'=4] {'wide'}, dimensions={0} | all-to-all | bytes 4718592 | tf_op jit(solution)/shard_map/all_to_all | solution.py:155
  43.9 2.9 %shard_map.60 = f32[128,8,128]{2,1,0:T(8,128)} custom-call(bf16[32,288,128]{2,1,0:T(8,128)(2,1)S(1)} %all_to_all.10.x_ref), custom_call_target="tpu_custom_call" | custom-call | tf_op jit(solution)/shard_map/pallas_call | solution.py:65
  46.8 5.7 %all-to-all-start.1 = ((f32[128,8,128]{2,1,0:T(8,128)}), f32[128,8,128]{2,1,0:T(8,128)S(1)}, u32[]{:S(2)}, u32[]{:S(2)}) async-start(f32[128,8,128]{2,1,0:T(8,128)} %shard_map.60), calls=%async_computation.1 | async-start | bytes 1048576 | tf_op jit(solution)/shard_map/all_to_all | solution.py:157
  52.5 0.0 copy-done
  52.6 14.1 %all-to-all-done.1.grams_ref = f32[128,8,128]{2,1,0:T(8,128)S(1)} async-done(((f32[128,8,128]{2,1,0:T(8,128)}), f32[128,8,128]{2,1,0:T(8,128)S(1)}, u32[]{:S(2)}, u32[]{:S(2)}) %all-to-all-start.1) | async-done | bytes 524320 | tf_op jit(solution)/shard_map/all_to_all | solution.py:157
  66.7 1.6 %shard_map.61 = (f32[288,128]{1,0:T(8,128)S(1)}, f32[8,128]{1,0:T(8,128)S(1)}) custom-call(f32[128,8,128]{2,1,0:T(8,128)S(1)} %all-to-all-done.1.grams_ref, f32[1,128]{1,0:T(1,128)S(1)} %pad_bitcast_fusion.counts_ref, bf16[32,288,128]{2,1,0:T(8,128)(2,1)S(1)} %all_to_all.10.x_ref), custom_call_target="tpu_custom_call" | custom-call | tf_op jit(solution)/shard_map/pallas_call | solution.py:122
  68.3 0.5 slice.6
  69.4 1.3 %conditional.1 = (f32[288,128]{1,0:T(8,128)S(1)}, f32[]{:T(128)}) conditional(s32[]{:T(128)} %bitcast.3, (f32[32]{0:T(128)S(1)}, bf16[32,288,128]{2,1,0:T(8,128)(2,1)S(1)}) %tuple.16, (f32[8,128]{1,0:T(8,128)S(1)}, f32[288,128]{1,0:T(8,128)S(1)}) %tuple.17), branch_computations={%region_0.18_spmd, %region_18.19_spmd} | conditional | flops 30561148 | bytes 17846776 | solution.py:159
  69.5 0.6 slice.4
  70.8 24.4 %all-gather.1 = f16[1179648]{0:T(1024)(128)(2,1)S(1)} all-gather(f16[36864]{0:T(1024)(128)(2,1)S(1)} %convert_bitcast_fusion), channel_id=1, replica_groups=mesh['wide'=32,'narrow'=4] {'wide'}, dimensions={0}, use_global_device_ids=true | all-gather | bytes 2433024 | tf_op jit(solution)/shard_map/all_gather | solution.py:161
  95.2 6.5 %fusion.14 = (f32[1179648]{0:T(1024)}, f32[1179648]{0:T(1024)}) fusion(f32[1179648]{0:T(1024)} %param.9, f32[]{:T(128)} %get-tuple-element.21, f16[1179648]{0:T(1024)(128)(2,1)S(1)} %all-gather.1, f32[1179648]{0:T(1024)} %param.8), kind=kLoop, calls=%fused_computation.34 | loop fusion | flops 5898240 | bytes 21233668 | tf_op jit(solution)/shard_map/add | solution.py:163
  (3 shorter events, 0.0 us)
Async XLA Ops:
  3.2 49.4 %copy-start = (s32[32]{0:T(128)S(1)}, s32[32]{0:T(128)}, u32[]{:S(2)}) copy-start(s32[32]{0:T(128)} %param.7) | copy-start | bytes 388
  46.8 19.9 %all-to-all-start.1 = ((f32[128,8,128]{2,1,0:T(8,128)}), f32[128,8,128]{2,1,0:T(8,128)S(1)}, u32[]{:S(2)}, u32[]{:S(2)}) async-start(f32[128,8,128]{2,1,0:T(8,128)} %shard_map.60), calls=%async_computation.1 | async-start | bytes 1048576 | tf_op jit(solution)/shard_map/all_to_all | solution.py:157

commit v2 on v1

v2 whole, which is shorter than its diff:
```python
import jax
import jax.numpy as jnp
from jax import lax
from jax.experimental import pallas as pl
from jax.experimental.pallas import tpu as pltpu
from jax.sharding import PartitionSpec as P

ITERS = 3


NU_SQUARE = 1.0
MOMENTUM_RATE = 0.9
SERVER_RATE = 1.0

LANES = 128
GROUP = 16
BLOCK = 48
SHARED = 24
TOP = 32000.0
SMALLEST = 2.0**-100
SAFE_SHARE = 1.0 / 256.0
VMEM = 24 << 20
SIDE = 4


def params(**more):
    return pltpu.CompilerParams(vmem_limit_bytes=VMEM, **more)


def pack_kernel(flat_ref, packed_ref):
    packed_ref[...] = flat_ref[...].reshape(packed_ref.shape)


def pack(deltas, clients):
    entries = deltas.shape[1]
    rows = entries // LANES
    steps = 2
    packed = pl.pallas_call(
        pack_kernel,
        grid=(steps,),
        in_specs=[pl.BlockSpec((1, entries // steps), lambda i: (0, i))],
        out_specs=pl.BlockSpec((rows // steps, LANES), lambda i: (i, 0)),
        out_shape=jax.ShapeDtypeStruct((rows, LANES), deltas.dtype),
        compiler_params=params(),
    )(deltas)
    return packed.reshape(clients, rows // clients, LANES)


def gram_kernel(x_ref, out_ref):
    clients, rows, _ = x_ref.shape
    wide = clients * GROUP
    y = jnp.concatenate(
        [x_ref[:, pl.ds(GROUP * k, GROUP), :].reshape(wide, LANES) for k in range(rows // GROUP)], axis=1
    )
    products = lax.dot_general(y, y, (((1,), (1,)), ((), ())), preferred_element_type=jnp.float32)
    row = lax.broadcasted_iota(jnp.int32, products.shape, 0)
    column = lax.broadcasted_iota(jnp.int32, products.shape, 1)
    products = jnp.where((row & (GROUP - 1)) == (column & (GROUP - 1)), products, 0.0)
    summed = products.reshape(clients, GROUP, wide).sum(axis=1)
    owner = lax.broadcasted_iota(jnp.int32, (wide, LANES), 0) // GROUP
    lane = lax.broadcasted_iota(jnp.int32, (wide, LANES), 1)
    place = jnp.where((lane & (clients - 1)) == owner, 1.0, 0.0)
    gram = jnp.dot(summed, place, precision=lax.Precision.HIGHEST, preferred_element_type=jnp.float32)
    row = lax.broadcasted_iota(jnp.int32, gram.shape, 0)
    lane = lax.broadcasted_iota(jnp.int32, gram.shape, 1)
    for j in range(out_ref.shape[1]):
        other = (lane - (4 * j + lane // clients)) & (clients - 1)
        diagonals = jnp.where(row == other, gram, 0.0).sum(axis=0, keepdims=True)
        out_ref[:, j] = jnp.broadcast_to(diagonals[None], (out_ref.shape[0], 1, LANES))


def gram_copies(x, copies):
    clients, rows, _ = x.shape
    return pl.pallas_call(
        gram_kernel,
        out_shape=jax.ShapeDtypeStruct((copies, clients // 8 + 1, 1, LANES), jnp.float32),
        compiler_params=params(),
    )(x)


def encode(total):
    values, exponents = [], []
    for at in range(0, BLOCK, SHARED):
        part = total[at : at + SHARED]
        largest = jnp.maximum(jnp.abs(part).max(axis=0, keepdims=True), SMALLEST)
        exponent = jnp.ceil(jnp.log2(largest))
        values.append(jnp.round(part * (TOP * jnp.exp2(-exponent))))
        exponents.append(exponent)
    return jnp.concatenate(values, axis=0).astype(jnp.int32).astype(jnp.int16), exponents


def encode_into(piece_ref, exponent_ref, rows, total_of):
    exponent_ref[...] = jnp.zeros_like(exponent_ref)

    def step(k, carry):
        at = pl.ds(pl.multiple_of(k * BLOCK, BLOCK), BLOCK)
        values, exponents = encode(total_of(at))
        piece_ref[at, :] = values
        for i, exponent in enumerate(exponents):
            exponent_ref[pl.ds(len(exponents) * k + i, 1), :] = exponent
        return carry

    lax.fori_loop(0, rows // BLOCK, step, 0)
    piece_ref[rows : rows + GROUP, :] = exponent_ref[...].astype(jnp.int32).astype(jnp.int16)


def encode_kernel(median_ref, piece_ref, exponent_ref):
    encode_into(piece_ref, exponent_ref, median_ref.shape[0], lambda at: median_ref[at, :])


def encoded(median):
    rows, _ = median.shape
    return pl.pallas_call(
        encode_kernel,
        out_shape=jax.ShapeDtypeStruct((rows + GROUP, LANES), jnp.int16),
        scratch_shapes=[pltpu.VMEM((GROUP, LANES), jnp.float32)],
        compiler_params=params(),
    )(median)


def median_kernel(grams_ref, counts_ref, x_ref, piece_ref, safe_ref, beta_ref, exponent_ref):
    clients, rows, _ = x_ref.shape
    summed = jnp.sum(grams_ref[...], axis=0)
    lane = lax.broadcasted_iota(jnp.int32, (clients, LANES), 1)
    row = lax.broadcasted_iota(jnp.int32, (clients, LANES), 0)
    behind = jnp.where(lane < clients, (lane - row) & (clients - 1), clients)
    half = jnp.zeros((clients, LANES), jnp.float32)
    for k in range(clients // 2 + 1):
        diagonal = summed[k // 4]
        if k % 4:
            diagonal = pltpu.roll(diagonal, LANES - clients * (k % 4), 1)
        half = jnp.where(behind == k, diagonal, half)
    identity = jnp.where(lane == row, 1.0, 0.0)
    turned = lax.dot_general(
        half,
        identity,
        (((0,), (0,)), ((), ())),
        precision=lax.Precision.HIGHEST,
        preferred_element_type=jnp.float32,
    )[:clients]
    gram = jnp.where(behind <= clients // 2, half, turned)
    gram = jnp.where(lane < clients, gram, 0.0)
    square = jnp.where(lane == row, gram, 0.0).sum(axis=0, keepdims=True)
    norm = jnp.sqrt(square)

    def as_column(values):
        return jnp.where(lane == row, values, 0.0).sum(axis=1, keepdims=True)

    counts = counts_ref[...]
    share = counts / counts.sum(axis=1, keepdims=True)
    beta = share
    safe = jnp.ones((1, 1), jnp.float32)
    for sweep in range(ITERS):
        column = as_column(beta)
        inner = (gram * column).sum(axis=0, keepdims=True)
        median_square = (inner * beta).sum(axis=1, keepdims=True)
        mean_norm = (norm * beta).sum(axis=1, keepdims=True)
        distance = square - 2.0 * inner + median_square + NU_SQUARE
        scale = norm + mean_norm
        margin = jnp.where(lane[:1] < clients, distance - SAFE_SHARE * (scale * scale), 1.0)
        safe = jnp.minimum(safe, margin.min(axis=1, keepdims=True))
        beta = share / jnp.sqrt(jnp.maximum(distance, NU_SQUARE))
        beta = beta / beta.sum(axis=1, keepdims=True)
    safe_ref[0] = jnp.where(safe[0, 0] > 0.0, 1, 0)
    beta_ref[...] = jnp.broadcast_to(as_column(beta), beta_ref.shape)

    def total_of(at):
        total = jnp.zeros((BLOCK, LANES), jnp.float32)
        for c in range(clients):
            total = total + beta_ref[c : c + 1, :] * x_ref[c, at, :].astype(jnp.float32)
        return total

    encode_into(piece_ref, exponent_ref, rows, total_of)


def median_of(grams, counts, x):
    clients, rows, _ = x.shape
    return pl.pallas_call(
        median_kernel,
        out_shape=(
            jax.ShapeDtypeStruct((rows + GROUP, LANES), jnp.int16),
            jax.ShapeDtypeStruct((1,), jnp.int32),
        ),
        out_specs=(pl.BlockSpec(memory_space=pltpu.VMEM), pl.BlockSpec(memory_space=pltpu.SMEM)),
        scratch_shapes=[pltpu.VMEM((clients, LANES), jnp.float32), pltpu.VMEM((GROUP, LANES), jnp.float32)],
        compiler_params=params(),
    )(grams, counts, x)


def update_kernel(parts, me_ref, *refs):
    quads = refs[: len(parts)]
    momentum_ref, weights_ref = refs[len(parts) : len(parts) + 2]
    new_momentum_ref, new_weights_ref, held, in_sem, out_sem = refs[-5:]
    rows = momentum_ref.shape[1]
    me = me_ref[0]
    x, z = me // (2 * SIDE), (me // 2) % SIDE

    def place(part, near_slot):
        flip, far_slot = parts[part]
        core = (me + flip) % 2
        near = jnp.where(core == 0, z, x)
        far = jnp.where(core == 0, x, z)
        near_at = (near + SIDE - near_slot) % SIDE
        far_at = (far + SIDE - far_slot) % SIDE
        return jnp.where(core == 0, far_at * SIDE + near_at, near_at * SIDE + far_at) * 2 + core

    def fetch(part, near_slot, i):
        slot = SIDE * part + near_slot
        source = (momentum_ref, weights_ref)[i]
        return pltpu.make_async_copy(source.at[place(part, near_slot)], held.at[slot, i], in_sem.at[slot, i])

    def store(part, near_slot, i):
        slot = SIDE * part + near_slot
        target = (new_momentum_ref, new_weights_ref)[i]
        return pltpu.make_async_copy(held.at[slot, i], target.at[place(part, near_slot)], out_sem.at[slot, i])

    def each(part, act):
        def step(near_slot, carry):
            for i in range(2):
                act(part, near_slot, i)
            return carry

        lax.fori_loop(0, SIDE, step, 0)

    for part in range(len(parts)):
        each(part, lambda *at: fetch(*at).start())
    for part in range(len(parts)):
        quad = quads[part]

        def work(near_slot, carry):
            slot = SIDE * part + near_slot
            for i in range(2):
                fetch(part, near_slot, i).wait()
            exponents = quad[near_slot, rows : rows + GROUP, :].astype(jnp.int32).astype(jnp.float32)
            scales = jnp.exp2(exponents) * (1.0 / TOP)
            for at in range(0, rows, BLOCK):
                values = quad[near_slot, at : at + BLOCK, :].astype(jnp.int32).astype(jnp.float32)
                for low in range(0, BLOCK, SHARED):
                    i = (at + low) // SHARED
                    block = pl.ds(at + low, SHARED)
                    median = values[low : low + SHARED] * scales[i : i + 1]
                    moved = MOMENTUM_RATE * held[slot, 0, block, :] + median
                    held[slot, 0, block, :] = moved
                    held[slot, 1, block, :] = held[slot, 1, block, :] + SERVER_RATE * moved
            for i in range(2):
                store(part, near_slot, i).start()
            return carry

        lax.fori_loop(0, SIDE, work, 0)
    for part in range(len(parts)):
        each(part, lambda *at: store(*at).wait())


def update(parts, me, quads, momentum, weights, made=()):
    pieces, rows, _ = momentum.shape
    vmem, hbm = pl.BlockSpec(memory_space=pltpu.VMEM), pl.BlockSpec(memory_space=pltpu.HBM)
    shape = pltpu.HBM(momentum.shape, momentum.dtype)
    in_hbm = [pltpu.with_memory_space_constraint(array, pltpu.HBM) for array in (momentum, weights, *made)]
    slots = SIDE * len(parts)
    return pl.pallas_call(
        lambda *refs: update_kernel(parts, *refs),
        in_specs=[pl.BlockSpec(memory_space=pltpu.SMEM)] + [vmem] * len(quads) + [hbm] * len(in_hbm),
        out_specs=(hbm, hbm),
        out_shape=(shape, shape),
        scratch_shapes=[
            pltpu.VMEM((slots, 2, rows, LANES), jnp.float32),
            pltpu.SemaphoreType.DMA((slots, 2)),
            pltpu.SemaphoreType.DMA((slots, 2)),
        ],
        input_output_aliases={1 + len(quads) + 2 + i: i for i in range(len(made))},
        compiler_params=params(),
        cost_estimate=pl.CostEstimate(
            flops=slots * rows * LANES * 6, bytes_accessed=4 * slots * rows * LANES * 4, transcendentals=0
        ),
    )(me, *quads, *in_hbm)


def along(step, shift):
    pairs = []
    for x in range(SIDE):
        for z in range(SIDE):
            for core in range(2):
                if (core == 0) == (step == 0):
                    to_x, to_z = x, (z + shift) % SIDE
                else:
                    to_x, to_z = (x + shift) % SIDE, z
                pairs.append(((x * SIDE + z) * 2 + core, (to_x * SIDE + to_z) * 2 + core))
    return pairs


def direct(x, counts):
    share = counts / jnp.sum(counts)
    wide = x.astype(jnp.float32)

    def weighted(coefficients):
        return jnp.sum(coefficients[:, None, None] * wide, axis=0)

    median = weighted(share)
    for sweep in range(ITERS):
        squared = lax.psum(jnp.sum(jnp.square(wide - median[None]), axis=(1, 2)), ("wide", "narrow"))
        beta = share / jnp.sqrt(squared + NU_SQUARE)
        median = weighted(beta) / jnp.sum(beta)
    return median


def shards(deltas, sample_counts, momentum, weights):
    clients = sample_counts.shape[0]
    counts = sample_counts.astype(jnp.float32)
    padded = jnp.pad(counts, (0, LANES - clients)).reshape(1, LANES)
    me = lax.axis_index("wide").astype(jnp.int32).reshape(1)
    x = lax.all_to_all(pack(deltas, clients), "wide", split_axis=0, concat_axis=0, tiled=True)
    devices = lax.axis_size(("wide", "narrow"))
    grams = lax.all_to_all(gram_copies(x, devices), ("wide", "narrow"), split_axis=0, concat_axis=0, tiled=True)
    flat = momentum.shape
    blocks = (clients, momentum.shape[0] // clients // LANES, LANES)
    momentum, weights = momentum.reshape(blocks), weights.reshape(blocks)
    piece, safe = median_of(grams, padded, x)

    def again(state):
        return jnp.int32(1), encoded(direct(x, counts))

    _, piece = lax.while_loop(lambda state: state[0] == 0, again, (safe[0], piece))

    near = [piece] + [lax.ppermute(piece, "wide", along(0, shift)) for shift in range(1, SIDE)]
    own = jnp.stack(near)
    ours = [own] + [lax.ppermute(own, "wide", along(1, shift)) for shift in range(1, SIDE)]
    across = [(i, i ^ 1) for i in range(2 * SIDE * SIDE)]
    mine = [lax.ppermute(own, "wide", along(1, shift)) for shift in (1, 3, 2)]
    theirs = lax.ppermute(own, "wide", across)
    made = update([(0, 0), (1, 0)], me, [own, theirs], momentum, weights)
    first, second, *made = lax.optimization_barrier((mine[0], mine[1], *made))
    theirs = [lax.ppermute(quad, "wide", across) for quad in (first, second)]
    made = update([(0, 1), (0, 3)], me, [first, second], momentum, weights, made)
    last, *made = lax.optimization_barrier((mine[2], *made))
    theirs = theirs + [lax.ppermute(last, "wide", across)]
    made = update([(1, 1), (1, 3), (0, 2)], me, [*theirs[:2], last], momentum, weights, made)
    new_momentum, new_weights = update([(1, 2)], me, theirs[2:], momentum, weights, made)
    return (new_weights.reshape(flat), new_momentum.reshape(flat))


def solution(mesh):
    placed = (P("wide", "narrow"), P(), P("narrow"), P("narrow"))
    return jax.shard_map(
        shards, mesh=mesh, in_specs=placed, out_specs=(P("narrow"), P("narrow")), check_vma=False
    )
```

time: 102 us -> 97.6 us (0.957)
  blocking collectives: 65.1 us -> 40.7 us
  Pallas kernels: 7.04 us -> 17 us
  starting transfers between devices: 5.74 us -> 15.7 us
  other arithmetic: 6.49 us -> 0.91 us
  waiting for transfers between devices: 14.1 us -> 18.9 us
  local copies, waits for them, and re-layouts: 1.12 us -> 2.34 us
    all_gather x1 -> x0, blocking collectives: 24.4 us -> none  [shards(): gathered = lax.all_gather(sent, 'wide', axis=0, tiled=True)]
    pallas_call x2 -> x6, Pallas kernels: 4.48 us -> 16.7 us  [the longest x4 11.4 us: update(): pl.pallas_call(lambda *refs: update_kernel(parts, *refs), in_specs=[pl.Bl...]
    ppermute x0 -> x10, starting transfers between devices: none -> 9.98 us  [the longest x3 3.63 us: shards(): mine = [lax.ppermute(own, 'wide', along(1, shift)) for shift in (1, 3, 2)]]
    ppermute x0 -> x10, waiting for transfers between devices: none -> 6.87 us  [the longest x3 3.46 us: shards(): mine = [lax.ppermute(own, 'wide', along(1, shift)) for shift in (1, 3, 2)]]
    add x1 -> x0, other arithmetic: 6.47 us -> none  [shards(): new_weights = weights + SERVER_RATE * new_momentum]
    unnamed x2 -> x4, local copies, waits for them, and re-layouts: 0.01 us -> 2.34 us
    pallas_call x1, Pallas kernels: 2.56 us -> 0.33 us  [pack(): pl.pallas_call(pack_kernel, grid=(steps,), in_specs=[pl.BlockSpec((1, ent...]
    all_to_all x1, waiting for transfers between devices: 14.1 us -> 12 us  [shards(): lax.all_to_all(gram_copies(x, devices), ('wide', 'narrow'), split_axis=0,...]
  transfers between devices with their start and end apart: 1 -> 11, of which waited for: 1 -> 5; matrix products, arithmetic and copies ran while one was open for 0% -> 0% of each run, Pallas kernels for 0% -> 9%
where the time goes in v2:
time: 97.6 us; the launch traced here: 97.1 us
  blocking collectives  40.7 us (42%)
  waiting for transfers between devices  18.9 us (19%)
  Pallas kernels  17 us (17%)
  starting transfers between devices  15.7 us (16%)
  local copies, waits for them, and re-layouts  2.34 us (2%)
    all_to_all x1, blocking collectives, shards(): lax.all_to_all(pack(deltas, clients), 'wide', split_axis=0, concat_axis=0...  40.7 us
    all_to_all x1, waiting for transfers between devices, shards(): lax.all_to_all(gram_copies(x, devices), ('wide', 'narrow'), split_axis=0,...  12 us
    pallas_call x4, Pallas kernels, update(): pl.pallas_call(lambda *refs: update_kernel(parts, *refs), in_specs=[pl.Bl...  11.4 us
    all_to_all x1, starting transfers between devices, shards(): lax.all_to_all(gram_copies(x, devices), ('wide', 'narrow'), split_axis=0,...  5.74 us
    ppermute x3, starting transfers between devices, shards(): mine = [lax.ppermute(own, 'wide', along(1, shift)) for shift in (1, 3, 2)]  3.63 us
    ppermute x3, waiting for transfers between devices, shards(): mine = [lax.ppermute(own, 'wide', along(1, shift)) for shift in (1, 3, 2)]  3.46 us
    ppermute x3, waiting for transfers between devices, shards(): lax.ppermute(piece, 'wide', along(0, shift))  3.41 us
    ppermute x3, starting transfers between devices, shards(): lax.ppermute(piece, 'wide', along(0, shift))  3.04 us
  transfers between devices with their start and end apart: 11, of which 5 were waited for; matrix products, arithmetic and copies ran while one was open for 0% of the time, Pallas kernels for 9%

profile of v2, /device:TPU:1, one launch (start us, length us, event | category | flops | bytes accessed | tf_op | source)
XLA Modules:
  0.0 97.1 jit_solution(4465158853937777221)
XLA Ops:
  0.6 2.3 %copy-done = bf16[1,1179648]{1,0:T(2,128)(2,1)S(1)} copy-done((bf16[1,1179648]{1,0:T(2,128)(2,1)S(1)}, bf16[1,1179648]{1,0:T(2,128)(2,1)}, u32[]{:S(2)}) %copy-start) | copy-done | bytes 2359320
  3.0 0.3 shard_map.59
  3.3 0.0 copy-start.1
  3.3 40.7 %all_to_all.10.x_ref = bf16[32,288,128]{2,1,0:T(8,128)(2,1)S(1)} all-to-all(bf16[32,288,128]{2,1,0:T(8,128)(2,1)S(1)} %bitcast.13), channel_id=1, replica_groups=mesh['wide'=32,'narrow'=4] {'wide'}, dimensions={0} | all-to-all | bytes 4718592 | tf_op jit(solution)/shard_map/all_to_all | solution.py:311
  44.0 2.6 %shard_map.60 = f32[128,5,1,128]{3,2,1,0:T(1,128)} custom-call(bf16[32,288,128]{2,1,0:T(8,128)(2,1)S(1)} %all_to_all.10.x_ref), custom_call_target="tpu_custom_call" | custom-call | tf_op jit(solution)/shard_map/pallas_call | solution.py:74
  46.7 5.7 %all-to-all-start.1 = ((f32[128,5,1,128]{3,2,1,0:T(1,128)}), f32[128,5,1,128]{3,2,1,0:T(1,128)S(1)}, u32[]{:S(2)}, u32[]{:S(2)}) async-start(f32[128,5,1,128]{3,2,1,0:T(1,128)} %shard_map.60), calls=%async_computation.1 | async-start | bytes 655360 | tf_op jit(solution)/shard_map/all_to_all | solution.py:313
  52.4 12.0 %all-to-all-done.1.grams_ref = f32[128,5,1,128]{3,2,1,0:T(1,128)S(1)} async-done(((f32[128,5,1,128]{3,2,1,0:T(1,128)}), f32[128,5,1,128]{3,2,1,0:T(1,128)S(1)}, u32[]{:S(2)}, u32[]{:S(2)}) %all-to-all-start.1) | async-done | bytes 327712 | tf_op jit(solution)/shard_map/all_to_all | solution.py:313
  64.4 2.6 %shard_map.61 = (s16[304,128]{1,0:T(8,128)(2,1)}, s32[1]{0:T(128)}) custom-call(f32[128,5,1,128]{3,2,1,0:T(1,128)S(1)} %all-to-all-done.1.grams_ref, f32[1,128]{1,0:T(1,128)S(1)} %pad_bitcast_fusion.counts_ref, bf16[32,288,128]{2,1,0:T(8,128)(2,1)S(1)} %all_to_all.10.x_ref), custom_call_target="tpu_custom_call" | custom-call | tf_op jit(solution)/shard_map/pallas_call | solution.py:178
  67.1 0.7 while.9
  67.7 0.4 collective-permute-start
  68.1 1.8 %collective-permute-start.1 = (s16[304,128]{1,0:T(8,128)(2,1)}, s16[304,128]{1,0:T(8,128)(2,1)S(1)}, u32[]{:S(2)}, u32[]{:S(2)}) collective-permute-start(s16[304,128]{1,0:T(8,128)(2,1)} %get-tuple-element.41), channel_id=1, source_target_pairs={{0,16},{4,68},{8,24},{12,76},{16,0},{20,84},{24,8},{28,92},{32,48}... | collective-permute-start | bytes 233480 | tf_op jit(solution)/shard_map/ppermute | solution.py:324
  69.9 0.9 collective-permute-start.2
  70.8 2.7 %collective-permute-done = s16[304,128]{1,0:T(8,128)(2,1)S(1)} collective-permute-done((s16[304,128]{1,0:T(8,128)(2,1)}, s16[304,128]{1,0:T(8,128)(2,1)S(1)}, u32[]{:S(2)}, u32[]{:S(2)}) %collective-permute-start) | collective-permute-done | bytes 77856 | tf_op jit(solution)/shard_map/ppermute | solution.py:324
  73.5 0.7 collective-permute-done.2
  74.2 0.9 pad_add_fusion.refs_1_
  75.1 1.5 %collective-permute-start.6 = (s16[4,304,128]{2,1,0:T(8,128)(2,1)S(1)}, s16[4,304,128]{2,1,0:T(8,128)(2,1)S(1)}, u32[]{:S(2)}, u32[]{:S(2)}) collective-permute-start(s16[4,304,128]{2,1,0:T(8,128)(2,1)S(1)} %pad_add_fusion.refs_1_), channel_id=1, source_target_pairs={{0,4},{4,0},{8,12},{12,8},{16,20},{20,16},{24,28},{28,24},{32,36},... | collective-permute-start | bytes 933896 | tf_op jit(solution)/shard_map/ppermute | solution.py:329
  76.6 0.9 collective-permute-start.4
  77.5 1.8 %collective-permute-start.5 = (s16[4,304,128]{2,1,0:T(8,128)(2,1)S(1)}, s16[4,304,128]{2,1,0:T(8,128)(2,1)S(1)}, u32[]{:S(2)}, u32[]{:S(2)}) collective-permute-start(s16[4,304,128]{2,1,0:T(8,128)(2,1)S(1)} %pad_add_fusion.refs_1_), channel_id=1, source_target_pairs={{0,96},{4,28},{8,104},{12,4},{16,112},{20,12},{24,120},{28,20},{32... | collective-permute-start | bytes 933896 | tf_op jit(solution)/shard_map/ppermute | solution.py:328
  79.2 1.0 collective-permute-start.3
  80.2 0.0 collective-permute-done.6.refs_2_
  80.2 2.8 %shard_map.62 = (f32[32,288,128]{2,1,0:T(8,128)}, f32[32,288,128]{2,1,0:T(8,128)}) custom-call(s32[1]{0:T(128)} %bitcast.refs_0_, s16[4,304,128]{2,1,0:T(8,128)(2,1)S(1)} %pad_add_fusion.refs_1_, s16[4,304,128]{2,1,0:T(8,128)(2,1)S(1)} %collective-permute-done.6.refs_2_, f32[32,288,128]{2,1,0:T(8,128)} %bitcast.14, f32[32,288,128]{2,1,0:T(8,128)} %bitcast.18), custom_call_target="tpu_custom_call" | custom-call | flops 1769472 | bytes 4718592 | tf_op jit(solution)/shard_map/pallas_call | solution.py:260
  83.0 0.9 collective-permute-done.4.refs_1_
  83.8 2.6 %collective-permute-done.5.refs_2_ = s16[4,304,128]{2,1,0:T(8,128)(2,1)S(1)} collective-permute-done((s16[4,304,128]{2,1,0:T(8,128)(2,1)S(1)}, s16[4,304,128]{2,1,0:T(8,128)(2,1)S(1)}, u32[]{:S(2)}, u32[]{:S(2)}) %collective-permute-start.5) | collective-permute-done | bytes 311328 | tf_op jit(solution)/shard_map/ppermute | solution.py:328
  86.4 1.2 %collective-permute-start.8 = (s16[4,304,128]{2,1,0:T(8,128)(2,1)S(1)}, s16[4,304,128]{2,1,0:T(8,128)(2,1)S(1)}, u32[]{:S(2)}, u32[]{:S(2)}) collective-permute-start(s16[4,304,128]{2,1,0:T(8,128)(2,1)S(1)} %collective-permute-done.4.refs_1_), channel_id=1, source_target_pairs={{0,4},{4,0},{8,12},{12,8},{16,20},{20,16},{24,28},{28,24},{32,36},... | collective-permute-start | bytes 933896 | tf_op jit(solution)/shard_map/ppermute | solution.py:332
  87.7 0.0 collective-permute-start.9
  87.7 2.8 %shard_map.63 = (f32[32,288,128]{2,1,0:T(8,128)}, f32[32,288,128]{2,1,0:T(8,128)}) custom-call(s32[1]{0:T(128)} %bitcast.refs_0_, s16[4,304,128]{2,1,0:T(8,128)(2,1)S(1)} %collective-permute-done.4.refs_1_, s16[4,304,128]{2,1,0:T(8,128)(2,1)S(1)} %collective-permute-done.5.refs_2_, ...), custom_call_target="tpu_custom_call", output_to_operand_aliasing={{0}: (5, {}), {1}: (6, {})} | custom-call | flops 1769472 | bytes 4718592 | tf_op jit(solution)/shard_map/pallas_call | solution.py:260
  90.4 0.0 collective-permute-done.3.refs_3_
  90.5 0.6 collective-permute-start.7
  91.0 0.0 collective-permute-done.8.refs_1_
  91.0 0.0 collective-permute-done.9.refs_2_
  91.0 3.6 %shard_map.64 = (f32[32,288,128]{2,1,0:T(8,128)}, f32[32,288,128]{2,1,0:T(8,128)}) custom-call(s32[1]{0:T(128)} %bitcast.refs_0_, s16[4,304,128]{2,1,0:T(8,128)(2,1)S(1)} %collective-permute-done.8.refs_1_, s16[4,304,128]{2,1,0:T(8,128)(2,1)S(1)} %collective-permute-done.9.refs_2_, ...), custom_call_target="tpu_custom_call", output_to_operand_aliasing={{0}: (6, {}), {1}: (7, {})} | custom-call | flops 2654208 | bytes 7077888 | tf_op jit(solution)/shard_map/pallas_call | solution.py:260
  94.7 2.3 %shard_map.65 = (f32[32,288,128]{2,1,0:T(8,128)}, f32[32,288,128]{2,1,0:T(8,128)}) custom-call(s32[1]{0:T(128)} %bitcast.refs_0_, s16[4,304,128]{2,1,0:T(8,128)(2,1)S(1)} %collective-permute-done.7.refs_1_, f32[32,288,128]{2,1,0:T(8,128)} %bitcast.17, f32[32,288,128]{2,1,0:T(8,128)} %bitcast.21, ...), custom_call_target="tpu_custom_call", output_to_operand_aliasing={{0}: (4, {}), {1}: (5, {})} | custom-call | flops 884736 | bytes 2359296 | tf_op jit(solution)/shard_map/pallas_call | solution.py:260
  (6 shorter events, 0.0 us)
Async XLA Ops:
  0.6 2.3 %copy-start = (bf16[1,1179648]{1,0:T(2,128)(2,1)S(1)}, bf16[1,1179648]{1,0:T(2,128)(2,1)}, u32[]{:S(2)}) copy-start(bf16[1,1179648]{1,0:T(2,128)(2,1)} %flat_ref.1) | copy-start | bytes 7077892
  3.3 49.1 %copy-start.1 = (s32[32]{0:T(128)S(1)}, s32[32]{0:T(128)}, u32[]{:S(2)}) copy-start(s32[32]{0:T(128)} %param.7) | copy-start | bytes 388
  46.7 17.8 %all-to-all-start.1 = ((f32[128,5,1,128]{3,2,1,0:T(1,128)}), f32[128,5,1,128]{3,2,1,0:T(1,128)S(1)}, u32[]{:S(2)}, u32[]{:S(2)}) async-start(f32[128,5,1,128]{3,2,1,0:T(1,128)} %shard_map.60), calls=%async_computation.1 | async-start | bytes 655360 | tf_op jit(solution)/shard_map/all_to_all | solution.py:313
  67.7 5.8 %collective-permute-start = (s16[304,128]{1,0:T(8,128)(2,1)}, s16[304,128]{1,0:T(8,128)(2,1)S(1)}, u32[]{:S(2)}, u32[]{:S(2)}) collective-permute-start(s16[304,128]{1,0:T(8,128)(2,1)} %get-tuple-element.41), channel_id=1, source_target_pairs={{0,8},{4,36},{8,16},{12,44},{16,24},{20,52},{24,0},{28,60},{32,40}... | collective-permute-start | bytes 233480 | tf_op jit(solution)/shard_map/ppermute | solution.py:324
  68.1 5.4 %collective-permute-start.1 = (s16[304,128]{1,0:T(8,128)(2,1)}, s16[304,128]{1,0:T(8,128)(2,1)S(1)}, u32[]{:S(2)}, u32[]{:S(2)}) collective-permute-start(s16[304,128]{1,0:T(8,128)(2,1)} %get-tuple-element.41), channel_id=1, source_target_pairs={{0,16},{4,68},{8,24},{12,76},{16,0},{20,84},{24,8},{28,92},{32,48}... | collective-permute-start | bytes 233480 | tf_op jit(solution)/shard_map/ppermute | solution.py:324
  69.9 4.3 %collective-permute-start.2 = (s16[304,128]{1,0:T(8,128)(2,1)}, s16[304,128]{1,0:T(8,128)(2,1)S(1)}, u32[]{:S(2)}, u32[]{:S(2)}) collective-permute-start(s16[304,128]{1,0:T(8,128)(2,1)} %get-tuple-element.41), channel_id=1, source_target_pairs={{0,24},{4,100},{8,0},{12,108},{16,8},{20,116},{24,16},{28,124},{32... | collective-permute-start | bytes 233480 | tf_op jit(solution)/shard_map/ppermute | solution.py:324
  75.1 5.1 %collective-permute-start.6 = (s16[4,304,128]{2,1,0:T(8,128)(2,1)S(1)}, s16[4,304,128]{2,1,0:T(8,128)(2,1)S(1)}, u32[]{:S(2)}, u32[]{:S(2)}) collective-permute-start(s16[4,304,128]{2,1,0:T(8,128)(2,1)S(1)} %pad_add_fusion.refs_1_), channel_id=1, source_target_pairs={{0,4},{4,0},{8,12},{12,8},{16,20},{20,16},{24,28},{28,24},{32,36},... | collective-permute-start | bytes 933896 | tf_op jit(solution)/shard_map/ppermute | solution.py:329
  76.6 7.3 %collective-permute-start.4 = (s16[4,304,128]{2,1,0:T(8,128)(2,1)S(1)}, s16[4,304,128]{2,1,0:T(8,128)(2,1)S(1)}, u32[]{:S(2)}, u32[]{:S(2)}) collective-permute-start(s16[4,304,128]{2,1,0:T(8,128)(2,1)S(1)} %pad_add_fusion.refs_1_), channel_id=1, source_target_pairs={{0,32},{4,12},{8,40},{12,20},{16,48},{20,28},{24,56},{28,4},{32,64... | collective-permute-start | bytes 933896 | tf_op jit(solution)/shard_map/ppermute | solution.py:328
  77.5 8.9 %collective-permute-start.5 = (s16[4,304,128]{2,1,0:T(8,128)(2,1)S(1)}, s16[4,304,128]{2,1,0:T(8,128)(2,1)S(1)}, u32[]{:S(2)}, u32[]{:S(2)}) collective-permute-start(s16[4,304,128]{2,1,0:T(8,128)(2,1)S(1)} %pad_add_fusion.refs_1_), channel_id=1, source_target_pairs={{0,96},{4,28},{8,104},{12,4},{16,112},{20,12},{24,120},{28,20},{32... | collective-permute-start | bytes 933896 | tf_op jit(solution)/shard_map/ppermute | solution.py:328
  79.2 11.2 %collective-permute-start.3 = (s16[4,304,128]{2,1,0:T(8,128)(2,1)S(1)}, s16[4,304,128]{2,1,0:T(8,128)(2,1)S(1)}, u32[]{:S(2)}, u32[]{:S(2)}) collective-permute-start(s16[4,304,128]{2,1,0:T(8,128)(2,1)S(1)} %pad_add_fusion.refs_1_), channel_id=1, source_target_pairs={{0,64},{4,20},{8,72},{12,28},{16,80},{20,4},{24,88},{28,12},{32,96... | collective-permute-start | bytes 933896 | tf_op jit(solution)/shard_map/ppermute | solution.py:328
  86.4 4.6 %collective-permute-start.8 = (s16[4,304,128]{2,1,0:T(8,128)(2,1)S(1)}, s16[4,304,128]{2,1,0:T(8,128)(2,1)S(1)}, u32[]{:S(2)}, u32[]{:S(2)}) collective-permute-start(s16[4,304,128]{2,1,0:T(8,128)(2,1)S(1)} %collective-permute-done.4.refs_1_), channel_id=1, source_target_pairs={{0,4},{4,0},{8,12},{12,8},{16,20},{20,16},{24,28},{28,24},{32,36},... | collective-permute-start | bytes 933896 | tf_op jit(solution)/shard_map/ppermute | solution.py:332
  87.7 3.4 %collective-permute-start.9 = (s16[4,304,128]{2,1,0:T(8,128)(2,1)S(1)}, s16[4,304,128]{2,1,0:T(8,128)(2,1)S(1)}, u32[]{:S(2)}, u32[]{:S(2)}) collective-permute-start(s16[4,304,128]{2,1,0:T(8,128)(2,1)S(1)} %collective-permute-done.5.refs_2_), channel_id=1, source_target_pairs={{0,4},{4,0},{8,12},{12,8},{16,20},{20,16},{24,28},{28,24},{32,36},... | collective-permute-start | bytes 933896 | tf_op jit(solution)/shard_map/ppermute | solution.py:332
  90.5 4.2 %collective-permute-start.7 = (s16[4,304,128]{2,1,0:T(8,128)(2,1)S(1)}, s16[4,304,128]{2,1,0:T(8,128)(2,1)S(1)}, u32[]{:S(2)}, u32[]{:S(2)}) collective-permute-start(s16[4,304,128]{2,1,0:T(8,128)(2,1)S(1)} %collective-permute-done.3.refs_3_), channel_id=1, source_target_pairs={{0,4},{4,0},{8,12},{12,8},{16,20},{20,16},{24,28},{28,24},{32,36},... | collective-permute-start | bytes 933896 | tf_op jit(solution)/shard_map/ppermute | solution.py:335

commit v3 on v2

--- a/solution.py
+++ b/solution.py
@@ -14,6 +14,7 @@
 
 LANES = 128
 GROUP = 16
+GRAM_ROWS = 8
 BLOCK = 48
 SHARED = 24
 TOP = 32000.0
@@ -48,16 +49,16 @@
 
 def gram_kernel(x_ref, out_ref):
     clients, rows, _ = x_ref.shape
-    wide = clients * GROUP
+    wide = clients * GRAM_ROWS
     y = jnp.concatenate(
-        [x_ref[:, pl.ds(GROUP * k, GROUP), :].reshape(wide, LANES) for k in range(rows // GROUP)], axis=1
+        [x_ref[:, pl.ds(GRAM_ROWS * k, GRAM_ROWS), :].reshape(wide, LANES) for k in range(rows // GRAM_ROWS)], axis=1
     )
     products = lax.dot_general(y, y, (((1,), (1,)), ((), ())), preferred_element_type=jnp.float32)
     row = lax.broadcasted_iota(jnp.int32, products.shape, 0)
     column = lax.broadcasted_iota(jnp.int32, products.shape, 1)
-    products = jnp.where((row & (GROUP - 1)) == (column & (GROUP - 1)), products, 0.0)
-    summed = products.reshape(clients, GROUP, wide).sum(axis=1)
-    owner = lax.broadcasted_iota(jnp.int32, (wide, LANES), 0) // GROUP
+    products = jnp.where((row & (GRAM_ROWS - 1)) == (column & (GRAM_ROWS - 1)), products, 0.0)
+    summed = products.reshape(clients, GRAM_ROWS, wide).sum(axis=1)
+    owner = lax.broadcasted_iota(jnp.int32, (wide, LANES), 0) // GRAM_ROWS
     lane = lax.broadcasted_iota(jnp.int32, (wide, LANES), 1)
     place = jnp.where((lane & (clients - 1)) == owner, 1.0, 0.0)
     gram = jnp.dot(summed, place, precision=lax.Precision.HIGHEST, preferred_element_type=jnp.float32)
@@ -102,20 +103,6 @@
 
     lax.fori_loop(0, rows // BLOCK, step, 0)
     piece_ref[rows : rows + GROUP, :] = exponent_ref[...].astype(jnp.int32).astype(jnp.int16)
-
-
-def encode_kernel(median_ref, piece_ref, exponent_ref):
-    encode_into(piece_ref, exponent_ref, median_ref.shape[0], lambda at: median_ref[at, :])
-
-
-def encoded(median):
-    rows, _ = median.shape
-    return pl.pallas_call(
-        encode_kernel,
-        out_shape=jax.ShapeDtypeStruct((rows + GROUP, LANES), jnp.int16),
-        scratch_shapes=[pltpu.VMEM((GROUP, LANES), jnp.float32)],
-        compiler_params=params(),
-    )(median)
 
 
 def median_kernel(grams_ref, counts_ref, x_ref, piece_ref, safe_ref, beta_ref, exponent_ref):
@@ -143,26 +130,27 @@
     square = jnp.where(lane == row, gram, 0.0).sum(axis=0, keepdims=True)
     norm = jnp.sqrt(square)
 
-    def as_column(values):
-        return jnp.where(lane == row, values, 0.0).sum(axis=1, keepdims=True)
-
+    square_column = jnp.where(lane == row, gram, 0.0).sum(axis=1, keepdims=True)
     counts = counts_ref[...]
-    share = counts / counts.sum(axis=1, keepdims=True)
-    beta = share
+    beta, beta_column = counts, jnp.where(lane == row, counts, 0.0).sum(axis=1, keepdims=True)
+    share, share_column = beta, beta_column
     safe = jnp.ones((1, 1), jnp.float32)
     for sweep in range(ITERS):
-        column = as_column(beta)
-        inner = (gram * column).sum(axis=0, keepdims=True)
-        median_square = (inner * beta).sum(axis=1, keepdims=True)
-        mean_norm = (norm * beta).sum(axis=1, keepdims=True)
-        distance = square - 2.0 * inner + median_square + NU_SQUARE
+        part = 1.0 / beta.sum(axis=1, keepdims=True)
+        inner = (gram * beta_column).sum(axis=0, keepdims=True)
+        inner_column = (gram * beta).sum(axis=1, keepdims=True)
+        median_square = (inner * beta).sum(axis=1, keepdims=True) * (part * part)
+        mean_norm = (norm * beta).sum(axis=1, keepdims=True) * part
+        distance = square - (2.0 * part) * inner + median_square + NU_SQUARE
+        distance_column = square_column - (2.0 * part) * inner_column + median_square + NU_SQUARE
         scale = norm + mean_norm
         margin = jnp.where(lane[:1] < clients, distance - SAFE_SHARE * (scale * scale), 1.0)
         safe = jnp.minimum(safe, margin.min(axis=1, keepdims=True))
         beta = share / jnp.sqrt(jnp.maximum(distance, NU_SQUARE))
-        beta = beta / beta.sum(axis=1, keepdims=True)
+        beta_column = share_column / jnp.sqrt(jnp.maximum(distance_column, NU_SQUARE))
+    beta_column = beta_column / beta.sum(axis=1, keepdims=True)
     safe_ref[0] = jnp.where(safe[0, 0] > 0.0, 1, 0)
-    beta_ref[...] = jnp.broadcast_to(as_column(beta), beta_ref.shape)
+    beta_ref[...] = jnp.broadcast_to(beta_column, beta_ref.shape)
 
     def total_of(at):
         total = jnp.zeros((BLOCK, LANES), jnp.float32)
@@ -269,9 +257,7 @@
         ],
         input_output_aliases={1 + len(quads) + 2 + i: i for i in range(len(made))},
         compiler_params=params(),
-        cost_estimate=pl.CostEstimate(
-            flops=slots * rows * LANES * 6, bytes_accessed=4 * slots * rows * LANES * 4, transcendentals=0
-        ),
+        cost_estimate=pl.CostEstimate(flops=1, bytes_accessed=1, transcendentals=0),
     )(me, *quads, *in_hbm)
 
 
@@ -300,7 +286,8 @@
         squared = lax.psum(jnp.sum(jnp.square(wide - median[None]), axis=(1, 2)), ("wide", "narrow"))
         beta = share / jnp.sqrt(squared + NU_SQUARE)
         median = weighted(beta) / jnp.sum(beta)
-    return median
+    copies = jnp.broadcast_to(median[None], x.shape)
+    return lax.all_to_all(copies, "wide", split_axis=0, concat_axis=0, tiled=True)
 
 
 def shards(deltas, sample_counts, momentum, weights):
@@ -316,25 +303,29 @@
     momentum, weights = momentum.reshape(blocks), weights.reshape(blocks)
     piece, safe = median_of(grams, padded, x)
 
-    def again(state):
-        return jnp.int32(1), encoded(direct(x, counts))
-
-    _, piece = lax.while_loop(lambda state: state[0] == 0, again, (safe[0], piece))
-
     near = [piece] + [lax.ppermute(piece, "wide", along(0, shift)) for shift in range(1, SIDE)]
     own = jnp.stack(near)
     ours = [own] + [lax.ppermute(own, "wide", along(1, shift)) for shift in range(1, SIDE)]
     across = [(i, i ^ 1) for i in range(2 * SIDE * SIDE)]
-    mine = [lax.ppermute(own, "wide", along(1, shift)) for shift in (1, 3, 2)]
     theirs = lax.ppermute(own, "wide", across)
+    first, second = (lax.ppermute(own, "wide", along(1, shift)) for shift in (1, 3))
     made = update([(0, 0), (1, 0)], me, [own, theirs], momentum, weights)
-    first, second, *made = lax.optimization_barrier((mine[0], mine[1], *made))
+    again_own, *made = lax.optimization_barrier((own, *made))
+    last = lax.ppermute(again_own, "wide", along(1, 2))
+    first, second, *made = lax.optimization_barrier((first, second, *made))
     theirs = [lax.ppermute(quad, "wide", across) for quad in (first, second)]
     made = update([(0, 1), (0, 3)], me, [first, second], momentum, weights, made)
-    last, *made = lax.optimization_barrier((mine[2], *made))
+    last, *made = lax.optimization_barrier((last, *made))
     theirs = theirs + [lax.ppermute(last, "wide", across)]
-    made = update([(1, 1), (1, 3), (0, 2)], me, [*theirs[:2], last], momentum, weights, made)
-    new_momentum, new_weights = update([(1, 2)], me, theirs[2:], momentum, weights, made)
+    made = update([(1, 1), (1, 3)], me, theirs[:2], momentum, weights, made)
+    new_momentum, new_weights = update([(0, 2), (1, 2)], me, [last, theirs[2]], momentum, weights, made)
+
+    def again(state):
+        new_momentum = MOMENTUM_RATE * momentum + direct(x, counts)
+        return jnp.int32(1), new_momentum, weights + SERVER_RATE * new_momentum
+
+    state = (safe[0], new_momentum, new_weights)
+    _, new_momentum, new_weights = lax.while_loop(lambda state: state[0] == 0, again, state)
     return (new_weights.reshape(flat), new_momentum.reshape(flat))
 
 

time: 97.6 us -> 94.9 us (0.972)
  Pallas kernels: 17 us -> 15.4 us
    ppermute x3, waiting for transfers between devices: 3.41 us -> 4.72 us  [shards(): lax.ppermute(piece, 'wide', along(0, shift))]
    ppermute x3, starting transfers between devices: 3.63 us -> 2.39 us  [the longest x2 1.47 us: shards(): lax.ppermute(own, 'wide', along(1, shift))]
    ppermute x3, waiting for transfers between devices: 3.46 us -> 2.47 us  [the longest x2 2.47 us: shards(): lax.ppermute(own, 'wide', along(1, shift))]
  transfers between devices with their start and end apart: 11 -> 11, of which waited for: 5 -> 6; matrix products, arithmetic and copies ran while one was open for 0% -> 0% of each run, Pallas kernels for 9% -> 9%
where the time goes in v3:
time: 94.9 us; the launch traced here: 94.5 us
  blocking collectives  40.7 us (43%)
  waiting for transfers between devices  19.2 us (20%)
  Pallas kernels  15.4 us (16%)
  starting transfers between devices  15.2 us (16%)
  local copies, waits for them, and re-layouts  2.34 us (2%)
    all_to_all x1, blocking collectives, shards(): lax.all_to_all(pack(deltas, clients), 'wide', split_axis=0, concat_axis=0...  40.7 us
    all_to_all x1, waiting for transfers between devices, shards(): lax.all_to_all(gram_copies(x, devices), ('wide', 'narrow'), split_axis=0,...  12 us
    pallas_call x4, Pallas kernels, update(): pl.pallas_call(lambda *refs: update_kernel(parts, *refs), in_specs=[pl.Bl...  11.1 us
    all_to_all x1, starting transfers between devices, shards(): lax.all_to_all(gram_copies(x, devices), ('wide', 'narrow'), split_axis=0,...  5.73 us
    ppermute x3, waiting for transfers between devices, shards(): lax.ppermute(piece, 'wide', along(0, shift))  4.72 us
    ppermute x2, waiting for transfers between devices, shards(): lax.ppermute(own, 'wide', along(1, shift))  2.47 us
    unnamed x4, local copies, waits for them, and re-layouts  2.34 us
    ppermute x3, starting transfers between devices, shards(): lax.ppermute(piece, 'wide', along(0, shift))  2.16 us
  transfers between devices with their start and end apart: 11, of which 6 were waited for; matrix products, arithmetic and copies ran while one was open for 0% of the time, Pallas kernels for 9%

profile of v3, /device:TPU:1, one launch (start us, length us, event | category | flops | bytes accessed | tf_op | source)
XLA Modules:
  0.0 94.5 jit_solution(737594033390658742)
XLA Ops:
  0.6 2.3 %copy-done = bf16[1,1179648]{1,0:T(2,128)(2,1)S(1)} copy-done((bf16[1,1179648]{1,0:T(2,128)(2,1)S(1)}, bf16[1,1179648]{1,0:T(2,128)(2,1)}, u32[]{:S(2)}) %copy-start) | copy-done | bytes 2359320
  3.0 0.3 shard_map.59
  3.3 0.0 copy-start.1
  3.3 40.7 %all_to_all.14.x_ref = bf16[32,288,128]{2,1,0:T(8,128)(2,1)S(1)} all-to-all(bf16[32,288,128]{2,1,0:T(8,128)(2,1)S(1)} %bitcast.13), channel_id=1, replica_groups=mesh['wide'=32,'narrow'=4] {'wide'}, dimensions={0} | all-to-all | bytes 4718592 | tf_op jit(solution)/shard_map/all_to_all | solution.py:298
  44.0 2.0 %shard_map.60 = f32[128,5,1,128]{3,2,1,0:T(1,128)} custom-call(bf16[32,288,128]{2,1,0:T(8,128)(2,1)S(1)} %all_to_all.14.x_ref), custom_call_target="tpu_custom_call" | custom-call | tf_op jit(solution)/shard_map/pallas_call | solution.py:75
  46.0 5.7 %all-to-all-start.2 = ((f32[128,5,1,128]{3,2,1,0:T(1,128)}), f32[128,5,1,128]{3,2,1,0:T(1,128)S(1)}, u32[]{:S(2)}, u32[]{:S(2)}) async-start(f32[128,5,1,128]{3,2,1,0:T(1,128)} %shard_map.60), calls=%async_computation.2 | async-start | bytes 655360 | tf_op jit(solution)/shard_map/all_to_all | solution.py:300
  51.8 12.0 %all-to-all-done.2.grams_ref = f32[128,5,1,128]{3,2,1,0:T(1,128)S(1)} async-done(((f32[128,5,1,128]{3,2,1,0:T(1,128)}), f32[128,5,1,128]{3,2,1,0:T(1,128)S(1)}, u32[]{:S(2)}, u32[]{:S(2)}) %all-to-all-start.2) | async-done | bytes 327712 | tf_op jit(solution)/shard_map/all_to_all | solution.py:300
  63.8 2.0 %shard_map.61 = (s16[304,128]{1,0:T(8,128)(2,1)S(1)}, s32[1]{0:T(128)}) custom-call(f32[128,5,1,128]{3,2,1,0:T(1,128)S(1)} %all-to-all-done.2.grams_ref, f32[1,128]{1,0:T(1,128)S(1)} %pad_bitcast_fusion.counts_ref, bf16[32,288,128]{2,1,0:T(8,128)(2,1)S(1)} %all_to_all.14.x_ref), custom_call_target="tpu_custom_call" | custom-call | tf_op jit(solution)/shard_map/pallas_call | solution.py:166
  65.8 0.9 collective-permute-start.2
  66.7 1.2 %collective-permute-start.1 = (s16[304,128]{1,0:T(8,128)(2,1)S(1)}, s16[304,128]{1,0:T(8,128)(2,1)S(1)}, u32[]{:S(2)}, u32[]{:S(2)}) collective-permute-start(s16[304,128]{1,0:T(8,128)(2,1)S(1)} %get-tuple-element.58), channel_id=1, source_target_pairs={{0,16},{4,68},{8,24},{12,76},{16,0},{20,84},{24,8},{28,92},{32,48}... | collective-permute-start | bytes 233480 | tf_op jit(solution)/shard_map/ppermute | solution.py:306
  68.0 0.0 collective-permute-start
  68.0 1.4 %collective-permute-done.2 = s16[304,128]{1,0:T(8,128)(2,1)S(1)} collective-permute-done((s16[304,128]{1,0:T(8,128)(2,1)S(1)}, s16[304,128]{1,0:T(8,128)(2,1)S(1)}, u32[]{:S(2)}, u32[]{:S(2)}) %collective-permute-start.2) | collective-permute-done | bytes 77856 | tf_op jit(solution)/shard_map/ppermute | solution.py:306
  69.4 2.1 %collective-permute-done.1 = s16[304,128]{1,0:T(8,128)(2,1)S(1)} collective-permute-done((s16[304,128]{1,0:T(8,128)(2,1)S(1)}, s16[304,128]{1,0:T(8,128)(2,1)S(1)}, u32[]{:S(2)}, u32[]{:S(2)}) %collective-permute-start.1) | collective-permute-done | bytes 77856 | tf_op jit(solution)/shard_map/ppermute | solution.py:306
  71.5 1.2 %collective-permute-done = s16[304,128]{1,0:T(8,128)(2,1)S(1)} collective-permute-done((s16[304,128]{1,0:T(8,128)(2,1)S(1)}, s16[304,128]{1,0:T(8,128)(2,1)S(1)}, u32[]{:S(2)}, u32[]{:S(2)}) %collective-permute-start) | collective-permute-done | bytes 77856 | tf_op jit(solution)/shard_map/ppermute | solution.py:306
  72.7 2.0 %collective-permute-start.3 = (s16[4,304,128]{2,1,0:T(8,128)(2,1)S(1)}, s16[4,304,128]{2,1,0:T(8,128)(2,1)S(1)}, u32[]{:S(2)}, u32[]{:S(2)}) collective-permute-start(s16[4,304,128]{2,1,0:T(8,128)(2,1)S(1)} %pad_add_fusion.refs_1_), channel_id=1, source_target_pairs={{0,4},{4,0},{8,12},{12,8},{16,20},{20,16},{24,28},{28,24},{32,36},... | collective-permute-start | bytes 933896 | tf_op jit(solution)/shard_map/ppermute | solution.py:310
  74.7 0.4 collective-permute-start.6
  75.1 1.1 %collective-permute-start.5 = (s16[4,304,128]{2,1,0:T(8,128)(2,1)S(1)}, s16[4,304,128]{2,1,0:T(8,128)(2,1)S(1)}, u32[]{:S(2)}, u32[]{:S(2)}) collective-permute-start(s16[4,304,128]{2,1,0:T(8,128)(2,1)S(1)} %pad_add_fusion.refs_1_), channel_id=1, source_target_pairs={{0,32},{4,12},{8,40},{12,20},{16,48},{20,28},{24,56},{28,4},{32,64... | collective-permute-start | bytes 933896 | tf_op jit(solution)/shard_map/ppermute | solution.py:311
  76.1 0.0 collective-permute-done.3.refs_2_
  76.1 2.8 %shard_map.62 = (f32[32,288,128]{2,1,0:T(8,128)}, f32[32,288,128]{2,1,0:T(8,128)}) custom-call(s32[1]{0:T(128)} %bitcast.3.refs_0_, s16[4,304,128]{2,1,0:T(8,128)(2,1)S(1)} %pad_add_fusion.refs_1_, s16[4,304,128]{2,1,0:T(8,128)(2,1)S(1)} %collective-permute-done.3.refs_2_, f32[32,288,128]{2,1,0:T(8,128)} %bitcast.15, f32[32,288,128]{2,1,0:T(8,128)} %bitcast.20), custom_call_target="tpu_custom_call" | custom-call | flops 1 | bytes 1 | tf_op jit(solution)/shard_map/pallas_call | solution.py:248
  78.9 0.9 collective-permute-start.4
  79.8 0.9 collective-permute-done.6.refs_2_
  80.7 1.6 %collective-permute-done.5.refs_1_ = s16[4,304,128]{2,1,0:T(8,128)(2,1)S(1)} collective-permute-done((s16[4,304,128]{2,1,0:T(8,128)(2,1)S(1)}, s16[4,304,128]{2,1,0:T(8,128)(2,1)S(1)}, u32[]{:S(2)}, u32[]{:S(2)}) %collective-permute-start.5) | collective-permute-done | bytes 311328 | tf_op jit(solution)/shard_map/ppermute | solution.py:311
  82.3 1.8 %collective-permute-start.8 = (s16[4,304,128]{2,1,0:T(8,128)(2,1)S(1)}, s16[4,304,128]{2,1,0:T(8,128)(2,1)S(1)}, u32[]{:S(2)}, u32[]{:S(2)}) collective-permute-start(s16[4,304,128]{2,1,0:T(8,128)(2,1)S(1)} %collective-permute-done.5.refs_1_), channel_id=1, source_target_pairs={{0,4},{4,0},{8,12},{12,8},{16,20},{20,16},{24,28},{28,24},{32,36},... | collective-permute-start | bytes 933896 | tf_op jit(solution)/shard_map/ppermute | solution.py:316
  84.1 0.0 collective-permute-start.9
  84.1 2.8 %shard_map.63 = (f32[32,288,128]{2,1,0:T(8,128)}, f32[32,288,128]{2,1,0:T(8,128)}) custom-call(s32[1]{0:T(128)} %bitcast.3.refs_0_, s16[4,304,128]{2,1,0:T(8,128)(2,1)S(1)} %collective-permute-done.5.refs_1_, s16[4,304,128]{2,1,0:T(8,128)(2,1)S(1)} %collective-permute-done.6.refs_2_, ...), custom_call_target="tpu_custom_call", output_to_operand_aliasing={{0}: (5, {}), {1}: (6, {})} | custom-call | flops 1 | bytes 1 | tf_op jit(solution)/shard_map/pallas_call | solution.py:248
  86.8 0.0 collective-permute-done.4.refs_1_
  86.9 1.2 %collective-permute-start.7 = (s16[4,304,128]{2,1,0:T(8,128)(2,1)S(1)}, s16[4,304,128]{2,1,0:T(8,128)(2,1)S(1)}, u32[]{:S(2)}, u32[]{:S(2)}) collective-permute-start(s16[4,304,128]{2,1,0:T(8,128)(2,1)S(1)} %collective-permute-done.4.refs_1_), channel_id=1, source_target_pairs={{0,4},{4,0},{8,12},{12,8},{16,20},{20,16},{24,28},{28,24},{32,36},... | collective-permute-start | bytes 933896 | tf_op jit(solution)/shard_map/ppermute | solution.py:319
  88.1 0.0 collective-permute-done.9.refs_2_
  88.1 2.8 %shard_map.64 = (f32[32,288,128]{2,1,0:T(8,128)}, f32[32,288,128]{2,1,0:T(8,128)}) custom-call(s32[1]{0:T(128)} %bitcast.3.refs_0_, s16[4,304,128]{2,1,0:T(8,128)(2,1)S(1)} %collective-permute-done.8.refs_1_, s16[4,304,128]{2,1,0:T(8,128)(2,1)S(1)} %collective-permute-done.9.refs_2_, ...), custom_call_target="tpu_custom_call", output_to_operand_aliasing={{0}: (5, {}), {1}: (6, {})} | custom-call | flops 1 | bytes 1 | tf_op jit(solution)/shard_map/pallas_call | solution.py:248
  90.8 0.0 collective-permute-done.7.refs_2_
  90.8 2.8 %shard_map.65 = (f32[32,288,128]{2,1,0:T(8,128)}, f32[32,288,128]{2,1,0:T(8,128)}) custom-call(s32[1]{0:T(128)} %bitcast.3.refs_0_, s16[4,304,128]{2,1,0:T(8,128)(2,1)S(1)} %collective-permute-done.4.refs_1_, s16[4,304,128]{2,1,0:T(8,128)(2,1)S(1)} %collective-permute-done.7.refs_2_, ...), custom_call_target="tpu_custom_call", output_to_operand_aliasing={{0}: (5, {}), {1}: (6, {})} | custom-call | flops 1 | bytes 1 | tf_op jit(solution)/shard_map/pallas_call | solution.py:248
  93.7 0.7 while.11
  (6 shorter events, 0.0 us)
Async XLA Ops:
  0.6 2.3 %copy-start = (bf16[1,1179648]{1,0:T(2,128)(2,1)S(1)}, bf16[1,1179648]{1,0:T(2,128)(2,1)}, u32[]{:S(2)}) copy-start(bf16[1,1179648]{1,0:T(2,128)(2,1)} %flat_ref.1) | copy-start | bytes 7077892
  3.3 48.4 %copy-start.1 = (s32[32]{0:T(128)S(1)}, s32[32]{0:T(128)}, u32[]{:S(2)}) copy-start(s32[32]{0:T(128)} %param.7) | copy-start | bytes 388
  46.0 17.8 %all-to-all-start.2 = ((f32[128,5,1,128]{3,2,1,0:T(1,128)}), f32[128,5,1,128]{3,2,1,0:T(1,128)S(1)}, u32[]{:S(2)}, u32[]{:S(2)}) async-start(f32[128,5,1,128]{3,2,1,0:T(1,128)} %shard_map.60), calls=%async_computation.2 | async-start | bytes 655360 | tf_op jit(solution)/shard_map/all_to_all | solution.py:300
  65.8 3.6 %collective-permute-start.2 = (s16[304,128]{1,0:T(8,128)(2,1)S(1)}, s16[304,128]{1,0:T(8,128)(2,1)S(1)}, u32[]{:S(2)}, u32[]{:S(2)}) collective-permute-start(s16[304,128]{1,0:T(8,128)(2,1)S(1)} %get-tuple-element.58), channel_id=1, source_target_pairs={{0,24},{4,100},{8,0},{12,108},{16,8},{20,116},{24,16},{28,124},{32... | collective-permute-start | bytes 233480 | tf_op jit(solution)/shard_map/ppermute | solution.py:306
  66.7 4.8 %collective-permute-start.1 = (s16[304,128]{1,0:T(8,128)(2,1)S(1)}, s16[304,128]{1,0:T(8,128)(2,1)S(1)}, u32[]{:S(2)}, u32[]{:S(2)}) collective-permute-start(s16[304,128]{1,0:T(8,128)(2,1)S(1)} %get-tuple-element.58), channel_id=1, source_target_pairs={{0,16},{4,68},{8,24},{12,76},{16,0},{20,84},{24,8},{28,92},{32,48}... | collective-permute-start | bytes 233480 | tf_op jit(solution)/shard_map/ppermute | solution.py:306
  68.0 4.7 %collective-permute-start = (s16[304,128]{1,0:T(8,128)(2,1)S(1)}, s16[304,128]{1,0:T(8,128)(2,1)S(1)}, u32[]{:S(2)}, u32[]{:S(2)}) collective-permute-start(s16[304,128]{1,0:T(8,128)(2,1)S(1)} %get-tuple-element.58), channel_id=1, source_target_pairs={{0,8},{4,36},{8,16},{12,44},{16,24},{20,52},{24,0},{28,60},{32,40}... | collective-permute-start | bytes 233480 | tf_op jit(solution)/shard_map/ppermute | solution.py:306
  72.7 3.4 %collective-permute-start.3 = (s16[4,304,128]{2,1,0:T(8,128)(2,1)S(1)}, s16[4,304,128]{2,1,0:T(8,128)(2,1)S(1)}, u32[]{:S(2)}, u32[]{:S(2)}) collective-permute-start(s16[4,304,128]{2,1,0:T(8,128)(2,1)S(1)} %pad_add_fusion.refs_1_), channel_id=1, source_target_pairs={{0,4},{4,0},{8,12},{12,8},{16,20},{20,16},{24,28},{28,24},{32,36},... | collective-permute-start | bytes 933896 | tf_op jit(solution)/shard_map/ppermute | solution.py:310
  74.7 6.0 %collective-permute-start.6 = (s16[4,304,128]{2,1,0:T(8,128)(2,1)S(1)}, s16[4,304,128]{2,1,0:T(8,128)(2,1)S(1)}, u32[]{:S(2)}, u32[]{:S(2)}) collective-permute-start(s16[4,304,128]{2,1,0:T(8,128)(2,1)S(1)} %pad_add_fusion.refs_1_), channel_id=1, source_target_pairs={{0,96},{4,28},{8,104},{12,4},{16,112},{20,12},{24,120},{28,20},{32... | collective-permute-start | bytes 933896 | tf_op jit(solution)/shard_map/ppermute | solution.py:311
  75.1 7.3 %collective-permute-start.5 = (s16[4,304,128]{2,1,0:T(8,128)(2,1)S(1)}, s16[4,304,128]{2,1,0:T(8,128)(2,1)S(1)}, u32[]{:S(2)}, u32[]{:S(2)}) collective-permute-start(s16[4,304,128]{2,1,0:T(8,128)(2,1)S(1)} %pad_add_fusion.refs_1_), channel_id=1, source_target_pairs={{0,32},{4,12},{8,40},{12,20},{16,48},{20,28},{24,56},{28,4},{32,64... | collective-permute-start | bytes 933896 | tf_op jit(solution)/shard_map/ppermute | solution.py:311
  78.9 7.9 %collective-permute-start.4 = (s16[4,304,128]{2,1,0:T(8,128)(2,1)S(1)}, s16[4,304,128]{2,1,0:T(8,128)(2,1)S(1)}, u32[]{:S(2)}, u32[]{:S(2)}) collective-permute-start(s16[4,304,128]{2,1,0:T(8,128)(2,1)S(1)} %pad_add_fusion.refs_1_), channel_id=1, source_target_pairs={{0,64},{4,20},{8,72},{12,28},{16,80},{20,4},{24,88},{28,12},{32,96... | collective-permute-start | bytes 933896 | tf_op jit(solution)/shard_map/ppermute | solution.py:314
  82.3 5.7 %collective-permute-start.8 = (s16[4,304,128]{2,1,0:T(8,128)(2,1)S(1)}, s16[4,304,128]{2,1,0:T(8,128)(2,1)S(1)}, u32[]{:S(2)}, u32[]{:S(2)}) collective-permute-start(s16[4,304,128]{2,1,0:T(8,128)(2,1)S(1)} %collective-permute-done.5.refs_1_), channel_id=1, source_target_pairs={{0,4},{4,0},{8,12},{12,8},{16,20},{20,16},{24,28},{28,24},{32,36},... | collective-permute-start | bytes 933896 | tf_op jit(solution)/shard_map/ppermute | solution.py:316
  84.1 4.0 %collective-permute-start.9 = (s16[4,304,128]{2,1,0:T(8,128)(2,1)S(1)}, s16[4,304,128]{2,1,0:T(8,128)(2,1)S(1)}, u32[]{:S(2)}, u32[]{:S(2)}) collective-permute-start(s16[4,304,128]{2,1,0:T(8,128)(2,1)S(1)} %collective-permute-done.6.refs_2_), channel_id=1, source_target_pairs={{0,4},{4,0},{8,12},{12,8},{16,20},{20,16},{24,28},{28,24},{32,36},... | collective-permute-start | bytes 933896 | tf_op jit(solution)/shard_map/ppermute | solution.py:316
  86.9 4.0 %collective-permute-start.7 = (s16[4,304,128]{2,1,0:T(8,128)(2,1)S(1)}, s16[4,304,128]{2,1,0:T(8,128)(2,1)S(1)}, u32[]{:S(2)}, u32[]{:S(2)}) collective-permute-start(s16[4,304,128]{2,1,0:T(8,128)(2,1)S(1)} %collective-permute-done.4.refs_1_), channel_id=1, source_target_pairs={{0,4},{4,0},{8,12},{12,8},{16,20},{20,16},{24,28},{28,24},{32,36},... | collective-permute-start | bytes 933896 | tf_op jit(solution)/shard_map/ppermute | solution.py:319

commit v4 on v3

--- a/solution.py
+++ b/solution.py
@@ -175,50 +175,65 @@
     )(grams, counts, x)
 
 
-def update_kernel(parts, me_ref, *refs):
-    quads = refs[: len(parts)]
-    momentum_ref, weights_ref = refs[len(parts) : len(parts) + 2]
-    new_momentum_ref, new_weights_ref, held, in_sem, out_sem = refs[-5:]
+def update_kernel(parts, ahead, given, first, me_ref, *refs):
+    quads, refs = refs[: len(parts)], refs[len(parts) :]
+    (momentum_ref, weights_ref), refs = refs[:2], refs[2:]
+    given_ref = refs[2] if given else None
+    if ahead:
+        new_momentum_ref, new_weights_ref, next_ref, held, in_sem, out_sem, next_sem = refs[-7:]
+    else:
+        new_momentum_ref, new_weights_ref, held, in_sem, out_sem = refs[-5:]
     rows = momentum_ref.shape[1]
     me = me_ref[0]
     x, z = me // (2 * SIDE), (me // 2) % SIDE
 
     def place(part, near_slot):
-        flip, far_slot = parts[part]
+        flip, far_slot = part
         core = (me + flip) % 2
-        near = jnp.where(core == 0, z, x)
-        far = jnp.where(core == 0, x, z)
+        near = jnp.where(core == 1, z, x)
+        far = jnp.where(core == 1, x, z)
         near_at = (near + SIDE - near_slot) % SIDE
         far_at = (far + SIDE - far_slot) % SIDE
-        return jnp.where(core == 0, far_at * SIDE + near_at, near_at * SIDE + far_at) * 2 + core
-
-    def fetch(part, near_slot, i):
-        slot = SIDE * part + near_slot
-        source = (momentum_ref, weights_ref)[i]
-        return pltpu.make_async_copy(source.at[place(part, near_slot)], held.at[slot, i], in_sem.at[slot, i])
-
-    def store(part, near_slot, i):
-        slot = SIDE * part + near_slot
+        return jnp.where(core == 1, far_at * SIDE + near_at, near_at * SIDE + far_at) * 2 + core
+
+    def copies(group, to_ref, sem):
+        def fetch(k, near_slot, i):
+            slot = SIDE * k + near_slot
+            source = (momentum_ref, weights_ref)[i]
+            return pltpu.make_async_copy(source.at[place(group[k], near_slot)], to_ref.at[slot, i], sem.at[slot, i])
+
+        return fetch
+
+    def store(k, near_slot, i):
+        slot = SIDE * k + near_slot
         target = (new_momentum_ref, new_weights_ref)[i]
-        return pltpu.make_async_copy(held.at[slot, i], target.at[place(part, near_slot)], out_sem.at[slot, i])
-
-    def each(part, act):
+        return pltpu.make_async_copy(held.at[slot, i], target.at[place(parts[k], near_slot)], out_sem.at[slot, i])
+
+    def each(k, act):
         def step(near_slot, carry):
             for i in range(2):
-                act(part, near_slot, i)
+                act(k, near_slot, i)
             return carry
 
         lax.fori_loop(0, SIDE, step, 0)
 
-    for part in range(len(parts)):
-        each(part, lambda *at: fetch(*at).start())
-    for part in range(len(parts)):
-        quad = quads[part]
+    fetch = copies(parts, held, in_sem)
+    if not given:
+        for k in range(len(parts)):
+            each(k, lambda *at: fetch(*at).start())
+    if ahead:
+        fetch_next = copies(ahead, next_ref, next_sem)
+        for k in range(len(ahead)):
+            each(k, lambda *at: fetch_next(*at).start())
+    source_ref, first = (given_ref, SIDE * first) if given else (held, 0)
+    for k in range(len(parts)):
+        quad = quads[k]
 
         def work(near_slot, carry):
-            slot = SIDE * part + near_slot
-            for i in range(2):
-                fetch(part, near_slot, i).wait()
+            slot = SIDE * k + near_slot
+            if not given:
+                for i in range(2):
+                    fetch(k, near_slot, i).wait()
             exponents = quad[near_slot, rows : rows + GROUP, :].astype(jnp.int32).astype(jnp.float32)
             scales = jnp.exp2(exponents) * (1.0 / TOP)
             for at in range(0, rows, BLOCK):
@@ -227,38 +242,43 @@
                     i = (at + low) // SHARED
                     block = pl.ds(at + low, SHARED)
                     median = values[low : low + SHARED] * scales[i : i + 1]
-                    moved = MOMENTUM_RATE * held[slot, 0, block, :] + median
+                    moved = MOMENTUM_RATE * source_ref[first + slot, 0, block, :] + median
                     held[slot, 0, block, :] = moved
-                    held[slot, 1, block, :] = held[slot, 1, block, :] + SERVER_RATE * moved
+                    held[slot, 1, block, :] = source_ref[first + slot, 1, block, :] + SERVER_RATE * moved
             for i in range(2):
-                store(part, near_slot, i).start()
+                store(k, near_slot, i).start()
             return carry
 
         lax.fori_loop(0, SIDE, work, 0)
-    for part in range(len(parts)):
-        each(part, lambda *at: store(*at).wait())
-
-
-def update(parts, me, quads, momentum, weights, made=()):
+    if ahead:
+        for k in range(len(ahead)):
+            each(k, lambda *at: fetch_next(*at).wait())
+    for k in range(len(parts)):
+        each(k, lambda *at: store(*at).wait())
+
+
+def update(parts, me, quads, momentum, weights, made=(), ahead=(), given=None, first=0):
     pieces, rows, _ = momentum.shape
     vmem, hbm = pl.BlockSpec(memory_space=pltpu.VMEM), pl.BlockSpec(memory_space=pltpu.HBM)
     shape = pltpu.HBM(momentum.shape, momentum.dtype)
     in_hbm = [pltpu.with_memory_space_constraint(array, pltpu.HBM) for array in (momentum, weights, *made)]
-    slots = SIDE * len(parts)
+    in_vmem = [] if given is None else [pltpu.with_memory_space_constraint(given, pltpu.VMEM)]
+    slots, next_slots = SIDE * len(parts), SIDE * len(ahead)
+    pair = (2, rows, LANES)
+    sems = pltpu.SemaphoreType.DMA((slots, 2))
+    more = bool(ahead)
     return pl.pallas_call(
-        lambda *refs: update_kernel(parts, *refs),
-        in_specs=[pl.BlockSpec(memory_space=pltpu.SMEM)] + [vmem] * len(quads) + [hbm] * len(in_hbm),
-        out_specs=(hbm, hbm),
-        out_shape=(shape, shape),
-        scratch_shapes=[
-            pltpu.VMEM((slots, 2, rows, LANES), jnp.float32),
-            pltpu.SemaphoreType.DMA((slots, 2)),
-            pltpu.SemaphoreType.DMA((slots, 2)),
-        ],
+        lambda *refs: update_kernel(parts, ahead, given is not None, first, *refs),
+        in_specs=[pl.BlockSpec(memory_space=pltpu.SMEM)] + [vmem] * len(quads) + [hbm] * 2 + [hbm] * len(made)
+        + [vmem] * len(in_vmem),
+        out_specs=(hbm, hbm) + (vmem,) * more,
+        out_shape=(shape, shape) + (pltpu.VMEM((next_slots, *pair), jnp.float32),) * more,
+        scratch_shapes=[pltpu.VMEM((slots, *pair), jnp.float32), sems, sems]
+        + [pltpu.SemaphoreType.DMA((next_slots, 2))] * more,
         input_output_aliases={1 + len(quads) + 2 + i: i for i in range(len(made))},
         compiler_params=params(),
         cost_estimate=pl.CostEstimate(flops=1, bytes_accessed=1, transcendentals=0),
-    )(me, *quads, *in_hbm)
+    )(me, *quads, *in_hbm, *in_vmem)
 
 
 def along(step, shift):
@@ -266,7 +286,7 @@
     for x in range(SIDE):
         for z in range(SIDE):
             for core in range(2):
-                if (core == 0) == (step == 0):
+                if (core == 1) == (step == 0):
                     to_x, to_z = x, (z + shift) % SIDE
                 else:
                     to_x, to_z = (x + shift) % SIDE, z
@@ -314,11 +334,12 @@
     last = lax.ppermute(again_own, "wide", along(1, 2))
     first, second, *made = lax.optimization_barrier((first, second, *made))
     theirs = [lax.ppermute(quad, "wide", across) for quad in (first, second)]
-    made = update([(0, 1), (0, 3)], me, [first, second], momentum, weights, made)
+    rest = [(1, 1), (1, 3), (0, 2), (1, 2)]
+    *made, given = update([(0, 1), (0, 3)], me, [first, second], momentum, weights, made, ahead=rest)
     last, *made = lax.optimization_barrier((last, *made))
     theirs = theirs + [lax.ppermute(last, "wide", across)]
-    made = update([(1, 1), (1, 3)], me, theirs[:2], momentum, weights, made)
-    new_momentum, new_weights = update([(0, 2), (1, 2)], me, [last, theirs[2]], momentum, weights, made)
+    made = update(rest[:2], me, theirs[:2], momentum, weights, made, given=given)
+    new_momentum, new_weights = update(rest[2:], me, [last, theirs[2]], momentum, weights, made, given=given, first=2)
 
     def again(state):
         new_momentum = MOMENTUM_RATE * momentum + direct(x, counts)

time: 94.9 us -> 93.3 us (0.983)
  waiting for transfers between devices: 19.2 us -> 16.6 us
    ppermute x2, waiting for transfers between devices: 2.47 us -> 0.82 us  [shards(): lax.ppermute(own, 'wide', along(1, shift))]
    ppermute x3, waiting for transfers between devices: 4.72 us -> 3.48 us  [shards(): lax.ppermute(piece, 'wide', along(0, shift))]
    ppermute x2, starting transfers between devices: 1.47 us -> 2.68 us  [shards(): lax.ppermute(own, 'wide', along(1, shift))]
  transfers between devices with their start and end apart: 11 -> 11, of which waited for: 6 -> 5; matrix products, arithmetic and copies ran while one was open for 0% -> 0% of each run, Pallas kernels for 9% -> 10%
where the time goes in v4:
time: 93.3 us; the launch traced here: 92.5 us
  blocking collectives  40.7 us (44%)
  waiting for transfers between devices  16.6 us (18%)
  starting transfers between devices  16.1 us (17%)
  Pallas kernels  15.2 us (16%)
  local copies, waits for them, and re-layouts  2.34 us (3%)
    all_to_all x1, blocking collectives, shards(): lax.all_to_all(pack(deltas, clients), 'wide', split_axis=0, concat_axis=0...  40.7 us
    all_to_all x1, waiting for transfers between devices, shards(): lax.all_to_all(gram_copies(x, devices), ('wide', 'narrow'), split_axis=0,...  12 us
    pallas_call x4, Pallas kernels, update(): pl.pallas_call(lambda *refs: update_kernel(parts, ahead, given is not Non...  10.8 us
    all_to_all x1, starting transfers between devices, shards(): lax.all_to_all(gram_copies(x, devices), ('wide', 'narrow'), split_axis=0,...  5.73 us
    ppermute x3, waiting for transfers between devices, shards(): lax.ppermute(piece, 'wide', along(0, shift))  3.48 us
    ppermute x3, starting transfers between devices, shards(): lax.ppermute(piece, 'wide', along(0, shift))  2.74 us
    ppermute x2, starting transfers between devices, shards(): lax.ppermute(own, 'wide', along(1, shift))  2.68 us
    unnamed x4, local copies, waits for them, and re-layouts  2.34 us
  transfers between devices with their start and end apart: 11, of which 5 were waited for; matrix products, arithmetic and copies ran while one was open for 0% of the time, Pallas kernels for 10%

profile of v4, /device:TPU:1, one launch (start us, length us, event | category | flops | bytes accessed | tf_op | source)
XLA Modules:
  0.0 92.5 jit_solution(1918494311087382484)
XLA Ops:
  0.6 2.3 %copy-done = bf16[1,1179648]{1,0:T(2,128)(2,1)S(1)} copy-done((bf16[1,1179648]{1,0:T(2,128)(2,1)S(1)}, bf16[1,1179648]{1,0:T(2,128)(2,1)}, u32[]{:S(2)}) %copy-start) | copy-done | bytes 2359320
  3.0 0.3 shard_map.59
  3.3 0.0 copy-start.1
  3.3 40.7 %all_to_all.14.x_ref = bf16[32,288,128]{2,1,0:T(8,128)(2,1)S(1)} all-to-all(bf16[32,288,128]{2,1,0:T(8,128)(2,1)S(1)} %bitcast.13), channel_id=1, replica_groups=mesh['wide'=32,'narrow'=4] {'wide'}, dimensions={0} | all-to-all | bytes 4718592 | tf_op jit(solution)/shard_map/all_to_all | solution.py:318
  44.0 2.0 %shard_map.60 = f32[128,5,1,128]{3,2,1,0:T(1,128)} custom-call(bf16[32,288,128]{2,1,0:T(8,128)(2,1)S(1)} %all_to_all.14.x_ref), custom_call_target="tpu_custom_call" | custom-call | tf_op jit(solution)/shard_map/pallas_call | solution.py:75
  46.0 5.7 %all-to-all-start.2 = ((f32[128,5,1,128]{3,2,1,0:T(1,128)}), f32[128,5,1,128]{3,2,1,0:T(1,128)S(1)}, u32[]{:S(2)}, u32[]{:S(2)}) async-start(f32[128,5,1,128]{3,2,1,0:T(1,128)} %shard_map.60), calls=%async_computation.2 | async-start | bytes 655360 | tf_op jit(solution)/shard_map/all_to_all | solution.py:320
  51.8 12.0 %all-to-all-done.2.grams_ref = f32[128,5,1,128]{3,2,1,0:T(1,128)S(1)} async-done(((f32[128,5,1,128]{3,2,1,0:T(1,128)}), f32[128,5,1,128]{3,2,1,0:T(1,128)S(1)}, u32[]{:S(2)}, u32[]{:S(2)}) %all-to-all-start.2) | async-done | bytes 327712 | tf_op jit(solution)/shard_map/all_to_all | solution.py:320
  63.8 2.0 %shard_map.61 = (s16[304,128]{1,0:T(8,128)(2,1)S(1)}, s32[1]{0:T(128)}) custom-call(f32[128,5,1,128]{3,2,1,0:T(1,128)S(1)} %all-to-all-done.2.grams_ref, f32[1,128]{1,0:T(1,128)S(1)} %pad_bitcast_fusion.counts_ref, bf16[32,288,128]{2,1,0:T(8,128)(2,1)S(1)} %all_to_all.14.x_ref), custom_call_target="tpu_custom_call" | custom-call | tf_op jit(solution)/shard_map/pallas_call | solution.py:166
  65.8 0.1 collective-permute-start
  65.9 1.6 %collective-permute-start.1 = (s16[304,128]{1,0:T(8,128)(2,1)S(1)}, s16[304,128]{1,0:T(8,128)(2,1)S(1)}, u32[]{:S(2)}, u32[]{:S(2)}) collective-permute-start(s16[304,128]{1,0:T(8,128)(2,1)S(1)} %get-tuple-element.59), channel_id=1, source_target_pairs={{0,64},{4,20},{8,72},{12,28},{16,80},{20,4},{24,88},{28,12},{32,96... | collective-permute-start | bytes 233480 | tf_op jit(solution)/shard_map/ppermute | solution.py:326
  67.4 1.1 %collective-permute-start.2 = (s16[304,128]{1,0:T(8,128)(2,1)S(1)}, s16[304,128]{1,0:T(8,128)(2,1)S(1)}, u32[]{:S(2)}, u32[]{:S(2)}) collective-permute-start(s16[304,128]{1,0:T(8,128)(2,1)S(1)} %get-tuple-element.59), channel_id=1, source_target_pairs={{0,96},{4,28},{8,104},{12,4},{16,112},{20,12},{24,120},{28,20},{32... | collective-permute-start | bytes 233480 | tf_op jit(solution)/shard_map/ppermute | solution.py:326
  68.6 2.9 %collective-permute-done = s16[304,128]{1,0:T(8,128)(2,1)S(1)} collective-permute-done((s16[304,128]{1,0:T(8,128)(2,1)S(1)}, s16[304,128]{1,0:T(8,128)(2,1)S(1)}, u32[]{:S(2)}, u32[]{:S(2)}) %collective-permute-start) | collective-permute-done | bytes 77856 | tf_op jit(solution)/shard_map/ppermute | solution.py:326
  71.5 0.0 collective-permute-done.1
  71.5 0.6 collective-permute-done.2
  72.1 1.5 %collective-permute-start.3 = (s16[4,304,128]{2,1,0:T(8,128)(2,1)S(1)}, s16[4,304,128]{2,1,0:T(8,128)(2,1)S(1)}, u32[]{:S(2)}, u32[]{:S(2)}) collective-permute-start(s16[4,304,128]{2,1,0:T(8,128)(2,1)S(1)} %pad_add_fusion.refs_1_), channel_id=1, source_target_pairs={{0,4},{4,0},{8,12},{12,8},{16,20},{20,16},{24,28},{28,24},{32,36},... | collective-permute-start | bytes 933896 | tf_op jit(solution)/shard_map/ppermute | solution.py:330
  73.5 0.9 collective-permute-start.5
  74.5 1.8 %collective-permute-start.6 = (s16[4,304,128]{2,1,0:T(8,128)(2,1)S(1)}, s16[4,304,128]{2,1,0:T(8,128)(2,1)S(1)}, u32[]{:S(2)}, u32[]{:S(2)}) collective-permute-start(s16[4,304,128]{2,1,0:T(8,128)(2,1)S(1)} %pad_add_fusion.refs_1_), channel_id=1, source_target_pairs={{0,24},{4,100},{8,0},{12,108},{16,8},{20,116},{24,16},{28,124},{32... | collective-permute-start | bytes 933896 | tf_op jit(solution)/shard_map/ppermute | solution.py:331
  76.2 0.0 collective-permute-done.3.refs_2_
  76.2 2.8 %shard_map.62 = (f32[32,288,128]{2,1,0:T(8,128)}, f32[32,288,128]{2,1,0:T(8,128)}) custom-call(s32[1]{0:T(128)} %bitcast.3.refs_0_, s16[4,304,128]{2,1,0:T(8,128)(2,1)S(1)} %pad_add_fusion.refs_1_, s16[4,304,128]{2,1,0:T(8,128)(2,1)S(1)} %collective-permute-done.3.refs_2_, f32[32,288,128]{2,1,0:T(8,128)} %bitcast.15, f32[32,288,128]{2,1,0:T(8,128)} %bitcast.20), custom_call_target="tpu_custom_call" | custom-call | flops 1 | bytes 1 | tf_op jit(solution)/shard_map/pallas_call | solution.py:270
  79.0 1.0 %collective-permute-start.4 = (s16[4,304,128]{2,1,0:T(8,128)(2,1)S(1)}, s16[4,304,128]{2,1,0:T(8,128)(2,1)S(1)}, u32[]{:S(2)}, u32[]{:S(2)}) collective-permute-start(s16[4,304,128]{2,1,0:T(8,128)(2,1)S(1)} %pad_add_fusion.refs_1_), channel_id=1, source_target_pairs={{0,16},{4,68},{8,24},{12,76},{16,0},{20,84},{24,8},{28,92},{32,48}... | collective-permute-start | bytes 933896 | tf_op jit(solution)/shard_map/ppermute | solution.py:334
  80.0 0.8 collective-permute-done.5.refs_1_
  80.8 0.9 %collective-permute-start.8 = (s16[4,304,128]{2,1,0:T(8,128)(2,1)S(1)}, s16[4,304,128]{2,1,0:T(8,128)(2,1)S(1)}, u32[]{:S(2)}, u32[]{:S(2)}) collective-permute-start(s16[4,304,128]{2,1,0:T(8,128)(2,1)S(1)} %collective-permute-done.5.refs_1_), channel_id=1, source_target_pairs={{0,4},{4,0},{8,12},{12,8},{16,20},{20,16},{24,28},{28,24},{32,36},... | collective-permute-start | bytes 933896 | tf_op jit(solution)/shard_map/ppermute | solution.py:336
  81.7 0.0 collective-permute-start.9
  81.7 4.6 %shard_map.63 = (f32[32,288,128]{2,1,0:T(8,128)}, f32[32,288,128]{2,1,0:T(8,128)}, f32[16,2,288,128]{3,2,1,0:T(8,128)S(1)}) custom-call(s32[1]{0:T(128)} %bitcast.3.refs_0_, s16[4,304,128]{2,1,0:T(8,128)(2,1)S(1)} %collective-permute-done.5.refs_1_, ...), custom_call_target="tpu_custom_call", output_to_operand_aliasing={{0}: (5, {}), {1}: (6, {})} | custom-call | flops 1 | bytes 1 | tf_op jit(solution)/shard_map/pallas_call | solution.py:270
  86.4 0.2 collective-permute-done.4.refs_1_
  86.6 1.5 %collective-permute-start.7 = (s16[4,304,128]{2,1,0:T(8,128)(2,1)S(1)}, s16[4,304,128]{2,1,0:T(8,128)(2,1)S(1)}, u32[]{:S(2)}, u32[]{:S(2)}) collective-permute-start(s16[4,304,128]{2,1,0:T(8,128)(2,1)S(1)} %collective-permute-done.4.refs_1_), channel_id=1, source_target_pairs={{0,4},{4,0},{8,12},{12,8},{16,20},{20,16},{24,28},{28,24},{32,36},... | collective-permute-start | bytes 933896 | tf_op jit(solution)/shard_map/ppermute | solution.py:340
  88.1 0.0 collective-permute-done.8.refs_1_
  88.1 0.0 collective-permute-done.9.refs_2_
  88.1 1.7 %shard_map.64 = (f32[32,288,128]{2,1,0:T(8,128)}, f32[32,288,128]{2,1,0:T(8,128)}) custom-call(s32[1]{0:T(128)} %bitcast.3.refs_0_, s16[4,304,128]{2,1,0:T(8,128)(2,1)S(1)} %collective-permute-done.8.refs_1_, s16[4,304,128]{2,1,0:T(8,128)(2,1)S(1)} %collective-permute-done.9.refs_2_, ...), custom_call_target="tpu_custom_call", output_to_operand_aliasing={{0}: (5, {}), {1}: (6, {})} | custom-call | flops 1 | bytes 1 | tf_op jit(solution)/shard_map/pallas_call | solution.py:270
  89.8 0.0 collective-permute-done.7.refs_2_
  89.9 1.7 %shard_map.65 = (f32[32,288,128]{2,1,0:T(8,128)}, f32[32,288,128]{2,1,0:T(8,128)}) custom-call(s32[1]{0:T(128)} %bitcast.3.refs_0_, s16[4,304,128]{2,1,0:T(8,128)(2,1)S(1)} %collective-permute-done.4.refs_1_, s16[4,304,128]{2,1,0:T(8,128)(2,1)S(1)} %collective-permute-done.7.refs_2_, ...), custom_call_target="tpu_custom_call", output_to_operand_aliasing={{0}: (5, {}), {1}: (6, {})} | custom-call | flops 1 | bytes 1 | tf_op jit(solution)/shard_map/pallas_call | solution.py:270
  91.6 0.7 while.11
  (6 shorter events, 0.0 us)
Async XLA Ops:
  0.6 2.3 %copy-start = (bf16[1,1179648]{1,0:T(2,128)(2,1)S(1)}, bf16[1,1179648]{1,0:T(2,128)(2,1)}, u32[]{:S(2)}) copy-start(bf16[1,1179648]{1,0:T(2,128)(2,1)} %flat_ref.1) | copy-start | bytes 7077892
  3.3 48.4 %copy-start.1 = (s32[32]{0:T(128)S(1)}, s32[32]{0:T(128)}, u32[]{:S(2)}) copy-start(s32[32]{0:T(128)} %param.7) | copy-start | bytes 388
  46.0 17.8 %all-to-all-start.2 = ((f32[128,5,1,128]{3,2,1,0:T(1,128)}), f32[128,5,1,128]{3,2,1,0:T(1,128)S(1)}, u32[]{:S(2)}, u32[]{:S(2)}) async-start(f32[128,5,1,128]{3,2,1,0:T(1,128)} %shard_map.60), calls=%async_computation.2 | async-start | bytes 655360 | tf_op jit(solution)/shard_map/all_to_all | solution.py:320
  65.8 5.7 %collective-permute-start = (s16[304,128]{1,0:T(8,128)(2,1)S(1)}, s16[304,128]{1,0:T(8,128)(2,1)S(1)}, u32[]{:S(2)}, u32[]{:S(2)}) collective-permute-start(s16[304,128]{1,0:T(8,128)(2,1)S(1)} %get-tuple-element.59), channel_id=1, source_target_pairs={{0,32},{4,12},{8,40},{12,20},{16,48},{20,28},{24,56},{28,4},{32,64... | collective-permute-start | bytes 233480 | tf_op jit(solution)/shard_map/ppermute | solution.py:326
  65.9 5.6 %collective-permute-start.1 = (s16[304,128]{1,0:T(8,128)(2,1)S(1)}, s16[304,128]{1,0:T(8,128)(2,1)S(1)}, u32[]{:S(2)}, u32[]{:S(2)}) collective-permute-start(s16[304,128]{1,0:T(8,128)(2,1)S(1)} %get-tuple-element.59), channel_id=1, source_target_pairs={{0,64},{4,20},{8,72},{12,28},{16,80},{20,4},{24,88},{28,12},{32,96... | collective-permute-start | bytes 233480 | tf_op jit(solution)/shard_map/ppermute | solution.py:326
  67.4 4.6 %collective-permute-start.2 = (s16[304,128]{1,0:T(8,128)(2,1)S(1)}, s16[304,128]{1,0:T(8,128)(2,1)S(1)}, u32[]{:S(2)}, u32[]{:S(2)}) collective-permute-start(s16[304,128]{1,0:T(8,128)(2,1)S(1)} %get-tuple-element.59), channel_id=1, source_target_pairs={{0,96},{4,28},{8,104},{12,4},{16,112},{20,12},{24,120},{28,20},{32... | collective-permute-start | bytes 233480 | tf_op jit(solution)/shard_map/ppermute | solution.py:326
  72.1 4.2 %collective-permute-start.3 = (s16[4,304,128]{2,1,0:T(8,128)(2,1)S(1)}, s16[4,304,128]{2,1,0:T(8,128)(2,1)S(1)}, u32[]{:S(2)}, u32[]{:S(2)}) collective-permute-start(s16[4,304,128]{2,1,0:T(8,128)(2,1)S(1)} %pad_add_fusion.refs_1_), channel_id=1, source_target_pairs={{0,4},{4,0},{8,12},{12,8},{16,20},{20,16},{24,28},{28,24},{32,36},... | collective-permute-start | bytes 933896 | tf_op jit(solution)/shard_map/ppermute | solution.py:330
  73.5 7.3 %collective-permute-start.5 = (s16[4,304,128]{2,1,0:T(8,128)(2,1)S(1)}, s16[4,304,128]{2,1,0:T(8,128)(2,1)S(1)}, u32[]{:S(2)}, u32[]{:S(2)}) collective-permute-start(s16[4,304,128]{2,1,0:T(8,128)(2,1)S(1)} %pad_add_fusion.refs_1_), channel_id=1, source_target_pairs={{0,8},{4,36},{8,16},{12,44},{16,24},{20,52},{24,0},{28,60},{32,40}... | collective-permute-start | bytes 933896 | tf_op jit(solution)/shard_map/ppermute | solution.py:331
  74.5 6.3 %collective-permute-start.6 = (s16[4,304,128]{2,1,0:T(8,128)(2,1)S(1)}, s16[4,304,128]{2,1,0:T(8,128)(2,1)S(1)}, u32[]{:S(2)}, u32[]{:S(2)}) collective-permute-start(s16[4,304,128]{2,1,0:T(8,128)(2,1)S(1)} %pad_add_fusion.refs_1_), channel_id=1, source_target_pairs={{0,24},{4,100},{8,0},{12,108},{16,8},{20,116},{24,16},{28,124},{32... | collective-permute-start | bytes 933896 | tf_op jit(solution)/shard_map/ppermute | solution.py:331
  79.0 7.6 %collective-permute-start.4 = (s16[4,304,128]{2,1,0:T(8,128)(2,1)S(1)}, s16[4,304,128]{2,1,0:T(8,128)(2,1)S(1)}, u32[]{:S(2)}, u32[]{:S(2)}) collective-permute-start(s16[4,304,128]{2,1,0:T(8,128)(2,1)S(1)} %pad_add_fusion.refs_1_), channel_id=1, source_target_pairs={{0,16},{4,68},{8,24},{12,76},{16,0},{20,84},{24,8},{28,92},{32,48}... | collective-permute-start | bytes 933896 | tf_op jit(solution)/shard_map/ppermute | solution.py:334
  80.8 7.3 %collective-permute-start.8 = (s16[4,304,128]{2,1,0:T(8,128)(2,1)S(1)}, s16[4,304,128]{2,1,0:T(8,128)(2,1)S(1)}, u32[]{:S(2)}, u32[]{:S(2)}) collective-permute-start(s16[4,304,128]{2,1,0:T(8,128)(2,1)S(1)} %collective-permute-done.5.refs_1_), channel_id=1, source_target_pairs={{0,4},{4,0},{8,12},{12,8},{16,20},{20,16},{24,28},{28,24},{32,36},... | collective-permute-start | bytes 933896 | tf_op jit(solution)/shard_map/ppermute | solution.py:336
  81.7 6.4 %collective-permute-start.9 = (s16[4,304,128]{2,1,0:T(8,128)(2,1)S(1)}, s16[4,304,128]{2,1,0:T(8,128)(2,1)S(1)}, u32[]{:S(2)}, u32[]{:S(2)}) collective-permute-start(s16[4,304,128]{2,1,0:T(8,128)(2,1)S(1)} %collective-permute-done.6.refs_2_), channel_id=1, source_target_pairs={{0,4},{4,0},{8,12},{12,8},{16,20},{20,16},{24,28},{28,24},{32,36},... | collective-permute-start | bytes 933896 | tf_op jit(solution)/shard_map/ppermute | solution.py:336
  86.6 3.2 %collective-permute-start.7 = (s16[4,304,128]{2,1,0:T(8,128)(2,1)S(1)}, s16[4,304,128]{2,1,0:T(8,128)(2,1)S(1)}, u32[]{:S(2)}, u32[]{:S(2)}) collective-permute-start(s16[4,304,128]{2,1,0:T(8,128)(2,1)S(1)} %collective-permute-done.4.refs_1_), channel_id=1, source_target_pairs={{0,4},{4,0},{8,12},{12,8},{16,20},{20,16},{24,28},{28,24},{32,36},... | collective-permute-start | bytes 933896 | tf_op jit(solution)/shard_map/ppermute | solution.py:340

commit v5 on v4

--- a/solution.py
+++ b/solution.py
@@ -332,14 +332,17 @@
     made = update([(0, 0), (1, 0)], me, [own, theirs], momentum, weights)
     again_own, *made = lax.optimization_barrier((own, *made))
     last = lax.ppermute(again_own, "wide", along(1, 2))
-    first, second, *made = lax.optimization_barrier((first, second, *made))
-    theirs = [lax.ppermute(quad, "wide", across) for quad in (first, second)]
-    rest = [(1, 1), (1, 3), (0, 2), (1, 2)]
-    *made, given = update([(0, 1), (0, 3)], me, [first, second], momentum, weights, made, ahead=rest)
+    rest = [(0, 3), (1, 1), (1, 3), (0, 2), (1, 2)]
+    first, *made = lax.optimization_barrier((first, *made))
+    theirs = [lax.ppermute(first, "wide", across)]
+    *made, given = update([(0, 1)], me, [first], momentum, weights, made, ahead=rest)
+    second, *made = lax.optimization_barrier((second, *made))
+    theirs = theirs + [lax.ppermute(second, "wide", across)]
+    made = update(rest[:1], me, [second], momentum, weights, made, given=given)
     last, *made = lax.optimization_barrier((last, *made))
     theirs = theirs + [lax.ppermute(last, "wide", across)]
-    made = update(rest[:2], me, theirs[:2], momentum, weights, made, given=given)
-    new_momentum, new_weights = update(rest[2:], me, [last, theirs[2]], momentum, weights, made, given=given, first=2)
+    made = update(rest[1:3], me, theirs[:2], momentum, weights, made, given=given, first=1)
+    new_momentum, new_weights = update(rest[3:], me, [last, theirs[2]], momentum, weights, made, given=given, first=3)
 
     def again(state):
         new_momentum = MOMENTUM_RATE * momentum + direct(x, counts)

time: 93.3 us -> 92.8 us (level)
    pallas_call x4 -> x5, Pallas kernels: 10.8 us -> 11.5 us  [update(): pl.pallas_call(lambda *refs: update_kernel(parts, ahead, given is not Non...]
  transfers between devices with their start and end apart: 11 -> 11, of which waited for: 5 -> 4; matrix products, arithmetic and copies ran while one was open for 0% -> 0% of each run, Pallas kernels for 10% -> 11%
where the time goes in v5:
time: 92.8 us; the launch traced here: 92.5 us
  blocking collectives  40.7 us (44%)
  waiting for transfers between devices  16.3 us (18%)
  Pallas kernels  15.8 us (17%)
  starting transfers between devices  15.6 us (17%)
  local copies, waits for them, and re-layouts  2.34 us (3%)
  between operations  0.94 us (1%)
    all_to_all x1, blocking collectives, shards(): lax.all_to_all(pack(deltas, clients), 'wide', split_axis=0, concat_axis=0...  40.7 us
    all_to_all x1, waiting for transfers between devices, shards(): lax.all_to_all(gram_copies(x, devices), ('wide', 'narrow'), split_axis=0,...  12 us
    pallas_call x5, Pallas kernels, update(): pl.pallas_call(lambda *refs: update_kernel(parts, ahead, given is not Non...  11.5 us
    all_to_all x1, starting transfers between devices, shards(): lax.all_to_all(gram_copies(x, devices), ('wide', 'narrow'), split_axis=0,...  5.73 us
    ppermute x3, waiting for transfers between devices, shards(): lax.ppermute(piece, 'wide', along(0, shift))  3.48 us
    ppermute x3, starting transfers between devices, shards(): lax.ppermute(piece, 'wide', along(0, shift))  2.74 us
    ppermute x2, starting transfers between devices, shards(): lax.ppermute(own, 'wide', along(1, shift))  2.68 us
    unnamed x4, local copies, waits for them, and re-layouts  2.34 us
  transfers between devices with their start and end apart: 11, of which 4 were waited for; matrix products, arithmetic and copies ran while one was open for 0% of the time, Pallas kernels for 11%

profile of v5, /device:TPU:1, one launch (start us, length us, event | category | flops | bytes accessed | tf_op | source)
XLA Modules:
  0.0 92.5 jit_solution(14600083987912822859)
XLA Ops:
  0.6 2.3 %copy-done = bf16[1,1179648]{1,0:T(2,128)(2,1)S(1)} copy-done((bf16[1,1179648]{1,0:T(2,128)(2,1)S(1)}, bf16[1,1179648]{1,0:T(2,128)(2,1)}, u32[]{:S(2)}) %copy-start) | copy-done | bytes 2359320
  3.0 0.3 shard_map.59
  3.3 0.0 copy-start.1
  3.3 40.7 %all_to_all.14.x_ref = bf16[32,288,128]{2,1,0:T(8,128)(2,1)S(1)} all-to-all(bf16[32,288,128]{2,1,0:T(8,128)(2,1)S(1)} %bitcast.13), channel_id=1, replica_groups=mesh['wide'=32,'narrow'=4] {'wide'}, dimensions={0} | all-to-all | bytes 4718592 | tf_op jit(solution)/shard_map/all_to_all | solution.py:318
  44.0 2.0 %shard_map.60 = f32[128,5,1,128]{3,2,1,0:T(1,128)} custom-call(bf16[32,288,128]{2,1,0:T(8,128)(2,1)S(1)} %all_to_all.14.x_ref), custom_call_target="tpu_custom_call" | custom-call | tf_op jit(solution)/shard_map/pallas_call | solution.py:75
  46.0 5.7 %all-to-all-start.2 = ((f32[128,5,1,128]{3,2,1,0:T(1,128)}), f32[128,5,1,128]{3,2,1,0:T(1,128)S(1)}, u32[]{:S(2)}, u32[]{:S(2)}) async-start(f32[128,5,1,128]{3,2,1,0:T(1,128)} %shard_map.60), calls=%async_computation.2 | async-start | bytes 655360 | tf_op jit(solution)/shard_map/all_to_all | solution.py:320
  51.8 12.0 %all-to-all-done.2.grams_ref = f32[128,5,1,128]{3,2,1,0:T(1,128)S(1)} async-done(((f32[128,5,1,128]{3,2,1,0:T(1,128)}), f32[128,5,1,128]{3,2,1,0:T(1,128)S(1)}, u32[]{:S(2)}, u32[]{:S(2)}) %all-to-all-start.2) | async-done | bytes 327712 | tf_op jit(solution)/shard_map/all_to_all | solution.py:320
  63.8 2.0 %shard_map.61 = (s16[304,128]{1,0:T(8,128)(2,1)S(1)}, s32[1]{0:T(128)}) custom-call(f32[128,5,1,128]{3,2,1,0:T(1,128)S(1)} %all-to-all-done.2.grams_ref, f32[1,128]{1,0:T(1,128)S(1)} %pad_bitcast_fusion.counts_ref, bf16[32,288,128]{2,1,0:T(8,128)(2,1)S(1)} %all_to_all.14.x_ref), custom_call_target="tpu_custom_call" | custom-call | tf_op jit(solution)/shard_map/pallas_call | solution.py:166
  65.8 0.1 collective-permute-start
  65.9 1.6 %collective-permute-start.1 = (s16[304,128]{1,0:T(8,128)(2,1)S(1)}, s16[304,128]{1,0:T(8,128)(2,1)S(1)}, u32[]{:S(2)}, u32[]{:S(2)}) collective-permute-start(s16[304,128]{1,0:T(8,128)(2,1)S(1)} %get-tuple-element.63), channel_id=1, source_target_pairs={{0,64},{4,20},{8,72},{12,28},{16,80},{20,4},{24,88},{28,12},{32,96... | collective-permute-start | bytes 233480 | tf_op jit(solution)/shard_map/ppermute | solution.py:326
  67.4 1.1 %collective-permute-start.2 = (s16[304,128]{1,0:T(8,128)(2,1)S(1)}, s16[304,128]{1,0:T(8,128)(2,1)S(1)}, u32[]{:S(2)}, u32[]{:S(2)}) collective-permute-start(s16[304,128]{1,0:T(8,128)(2,1)S(1)} %get-tuple-element.63), channel_id=1, source_target_pairs={{0,96},{4,28},{8,104},{12,4},{16,112},{20,12},{24,120},{28,20},{32... | collective-permute-start | bytes 233480 | tf_op jit(solution)/shard_map/ppermute | solution.py:326
  68.6 2.9 %collective-permute-done = s16[304,128]{1,0:T(8,128)(2,1)S(1)} collective-permute-done((s16[304,128]{1,0:T(8,128)(2,1)S(1)}, s16[304,128]{1,0:T(8,128)(2,1)S(1)}, u32[]{:S(2)}, u32[]{:S(2)}) %collective-permute-start) | collective-permute-done | bytes 77856 | tf_op jit(solution)/shard_map/ppermute | solution.py:326
  71.5 0.0 collective-permute-done.1
  71.5 0.6 collective-permute-done.2
  72.1 1.5 %collective-permute-start.3 = (s16[4,304,128]{2,1,0:T(8,128)(2,1)S(1)}, s16[4,304,128]{2,1,0:T(8,128)(2,1)S(1)}, u32[]{:S(2)}, u32[]{:S(2)}) collective-permute-start(s16[4,304,128]{2,1,0:T(8,128)(2,1)S(1)} %pad_add_fusion.refs_1_), channel_id=1, source_target_pairs={{0,4},{4,0},{8,12},{12,8},{16,20},{20,16},{24,28},{28,24},{32,36},... | collective-permute-start | bytes 933896 | tf_op jit(solution)/shard_map/ppermute | solution.py:330
  73.5 0.9 collective-permute-start.6
  74.5 1.8 %collective-permute-start.5 = (s16[4,304,128]{2,1,0:T(8,128)(2,1)S(1)}, s16[4,304,128]{2,1,0:T(8,128)(2,1)S(1)}, u32[]{:S(2)}, u32[]{:S(2)}) collective-permute-start(s16[4,304,128]{2,1,0:T(8,128)(2,1)S(1)} %pad_add_fusion.refs_1_), channel_id=1, source_target_pairs={{0,24},{4,100},{8,0},{12,108},{16,8},{20,116},{24,16},{28,124},{32... | collective-permute-start | bytes 933896 | tf_op jit(solution)/shard_map/ppermute | solution.py:331
  76.2 2.8 %shard_map.62 = (f32[32,288,128]{2,1,0:T(8,128)}, f32[32,288,128]{2,1,0:T(8,128)}) custom-call(s32[1]{0:T(128)} %bitcast.3.refs_0_, s16[4,304,128]{2,1,0:T(8,128)(2,1)S(1)} %pad_add_fusion.refs_1_, s16[4,304,128]{2,1,0:T(8,128)(2,1)S(1)} %collective-permute-done.3.refs_2_, f32[32,288,128]{2,1,0:T(8,128)} %bitcast.15, f32[32,288,128]{2,1,0:T(8,128)} %bitcast.21), custom_call_target="tpu_custom_call" | custom-call | flops 1 | bytes 1 | tf_op jit(solution)/shard_map/pallas_call | solution.py:270
  79.0 1.0 %collective-permute-start.4 = (s16[4,304,128]{2,1,0:T(8,128)(2,1)S(1)}, s16[4,304,128]{2,1,0:T(8,128)(2,1)S(1)}, u32[]{:S(2)}, u32[]{:S(2)}) collective-permute-start(s16[4,304,128]{2,1,0:T(8,128)(2,1)S(1)} %pad_add_fusion.refs_1_), channel_id=1, source_target_pairs={{0,16},{4,68},{8,24},{12,76},{16,0},{20,84},{24,8},{28,92},{32,48}... | collective-permute-start | bytes 933896 | tf_op jit(solution)/shard_map/ppermute | solution.py:334
  80.0 0.8 collective-permute-done.6.refs_1_
  80.8 0.9 %collective-permute-start.8 = (s16[4,304,128]{2,1,0:T(8,128)(2,1)S(1)}, s16[4,304,128]{2,1,0:T(8,128)(2,1)S(1)}, u32[]{:S(2)}, u32[]{:S(2)}) collective-permute-start(s16[4,304,128]{2,1,0:T(8,128)(2,1)S(1)} %collective-permute-done.6.refs_1_), channel_id=1, source_target_pairs={{0,4},{4,0},{8,12},{12,8},{16,20},{20,16},{24,28},{28,24},{32,36},... | collective-permute-start | bytes 933896 | tf_op jit(solution)/shard_map/ppermute | solution.py:337
  81.7 4.1 %shard_map.63 = (f32[32,288,128]{2,1,0:T(8,128)}, f32[32,288,128]{2,1,0:T(8,128)}, f32[20,2,288,128]{3,2,1,0:T(8,128)S(1)}) custom-call(s32[1]{0:T(128)} %bitcast.3.refs_0_, s16[4,304,128]{2,1,0:T(8,128)(2,1)S(1)} %collective-permute-done.6.refs_1_, f32[32,288,128]{2,1,0:T(8,128)} %bitcast.16, ...), custom_call_target="tpu_custom_call", output_to_operand_aliasing={{0}: (4, {}), {1}: (5, {})} | custom-call | flops 1 | bytes 1 | tf_op jit(solution)/shard_map/pallas_call | solution.py:270
  85.8 0.0 collective-permute-done.5.refs_1_
  85.8 0.1 collective-permute-start.9
  85.9 1.2 %shard_map.64 = (f32[32,288,128]{2,1,0:T(8,128)}, f32[32,288,128]{2,1,0:T(8,128)}) custom-call(s32[1]{0:T(128)} %bitcast.3.refs_0_, s16[4,304,128]{2,1,0:T(8,128)(2,1)S(1)} %collective-permute-done.5.refs_1_, f32[32,288,128]{2,1,0:T(8,128)} %bitcast.17, f32[32,288,128]{2,1,0:T(8,128)} %bitcast.23, ...), custom_call_target="tpu_custom_call", output_to_operand_aliasing={{0}: (4, {}), {1}: (5, {})} | custom-call | flops 1 | bytes 1 | tf_op jit(solution)/shard_map/pallas_call | solution.py:270
  87.1 0.0 collective-permute-done.4.refs_1_
  87.1 1.0 %collective-permute-start.7 = (s16[4,304,128]{2,1,0:T(8,128)(2,1)S(1)}, s16[4,304,128]{2,1,0:T(8,128)(2,1)S(1)}, u32[]{:S(2)}, u32[]{:S(2)}) collective-permute-start(s16[4,304,128]{2,1,0:T(8,128)(2,1)S(1)} %collective-permute-done.4.refs_1_), channel_id=1, source_target_pairs={{0,4},{4,0},{8,12},{12,8},{16,20},{20,16},{24,28},{28,24},{32,36},... | collective-permute-start | bytes 933896 | tf_op jit(solution)/shard_map/ppermute | solution.py:343
  88.1 0.0 collective-permute-done.9.refs_2_
  88.1 1.7 %shard_map.65 = (f32[32,288,128]{2,1,0:T(8,128)}, f32[32,288,128]{2,1,0:T(8,128)}) custom-call(s32[1]{0:T(128)} %bitcast.3.refs_0_, s16[4,304,128]{2,1,0:T(8,128)(2,1)S(1)} %collective-permute-done.8.refs_1_, s16[4,304,128]{2,1,0:T(8,128)(2,1)S(1)} %collective-permute-done.9.refs_2_, ...), custom_call_target="tpu_custom_call", output_to_operand_aliasing={{0}: (5, {}), {1}: (6, {})} | custom-call | flops 1 | bytes 1 | tf_op jit(solution)/shard_map/pallas_call | solution.py:270
  89.8 0.0 collective-permute-done.7.refs_2_
  89.8 1.7 %shard_map.66 = (f32[32,288,128]{2,1,0:T(8,128)}, f32[32,288,128]{2,1,0:T(8,128)}) custom-call(s32[1]{0:T(128)} %bitcast.3.refs_0_, s16[4,304,128]{2,1,0:T(8,128)(2,1)S(1)} %collective-permute-done.4.refs_1_, s16[4,304,128]{2,1,0:T(8,128)(2,1)S(1)} %collective-permute-done.7.refs_2_, ...), custom_call_target="tpu_custom_call", output_to_operand_aliasing={{0}: (5, {}), {1}: (6, {})} | custom-call | flops 1 | bytes 1 | tf_op jit(solution)/shard_map/pallas_call | solution.py:270
  91.6 0.7 while.11
  (7 shorter events, 0.0 us)
Async XLA Ops:
  0.6 2.3 %copy-start = (bf16[1,1179648]{1,0:T(2,128)(2,1)S(1)}, bf16[1,1179648]{1,0:T(2,128)(2,1)}, u32[]{:S(2)}) copy-start(bf16[1,1179648]{1,0:T(2,128)(2,1)} %flat_ref.1) | copy-start | bytes 7077892
  3.3 48.4 %copy-start.1 = (s32[32]{0:T(128)S(1)}, s32[32]{0:T(128)}, u32[]{:S(2)}) copy-start(s32[32]{0:T(128)} %param.7) | copy-start | bytes 388
  46.0 17.8 %all-to-all-start.2 = ((f32[128,5,1,128]{3,2,1,0:T(1,128)}), f32[128,5,1,128]{3,2,1,0:T(1,128)S(1)}, u32[]{:S(2)}, u32[]{:S(2)}) async-start(f32[128,5,1,128]{3,2,1,0:T(1,128)} %shard_map.60), calls=%async_computation.2 | async-start | bytes 655360 | tf_op jit(solution)/shard_map/all_to_all | solution.py:320
  65.8 5.7 %collective-permute-start = (s16[304,128]{1,0:T(8,128)(2,1)S(1)}, s16[304,128]{1,0:T(8,128)(2,1)S(1)}, u32[]{:S(2)}, u32[]{:S(2)}) collective-permute-start(s16[304,128]{1,0:T(8,128)(2,1)S(1)} %get-tuple-element.63), channel_id=1, source_target_pairs={{0,32},{4,12},{8,40},{12,20},{16,48},{20,28},{24,56},{28,4},{32,64... | collective-permute-start | bytes 233480 | tf_op jit(solution)/shard_map/ppermute | solution.py:326
  65.9 5.6 %collective-permute-start.1 = (s16[304,128]{1,0:T(8,128)(2,1)S(1)}, s16[304,128]{1,0:T(8,128)(2,1)S(1)}, u32[]{:S(2)}, u32[]{:S(2)}) collective-permute-start(s16[304,128]{1,0:T(8,128)(2,1)S(1)} %get-tuple-element.63), channel_id=1, source_target_pairs={{0,64},{4,20},{8,72},{12,28},{16,80},{20,4},{24,88},{28,12},{32,96... | collective-permute-start | bytes 233480 | tf_op jit(solution)/shard_map/ppermute | solution.py:326
  67.4 4.6 %collective-permute-start.2 = (s16[304,128]{1,0:T(8,128)(2,1)S(1)}, s16[304,128]{1,0:T(8,128)(2,1)S(1)}, u32[]{:S(2)}, u32[]{:S(2)}) collective-permute-start(s16[304,128]{1,0:T(8,128)(2,1)S(1)} %get-tuple-element.63), channel_id=1, source_target_pairs={{0,96},{4,28},{8,104},{12,4},{16,112},{20,12},{24,120},{28,20},{32... | collective-permute-start | bytes 233480 | tf_op jit(solution)/shard_map/ppermute | solution.py:326
  72.1 4.2 %collective-permute-start.3 = (s16[4,304,128]{2,1,0:T(8,128)(2,1)S(1)}, s16[4,304,128]{2,1,0:T(8,128)(2,1)S(1)}, u32[]{:S(2)}, u32[]{:S(2)}) collective-permute-start(s16[4,304,128]{2,1,0:T(8,128)(2,1)S(1)} %pad_add_fusion.refs_1_), channel_id=1, source_target_pairs={{0,4},{4,0},{8,12},{12,8},{16,20},{20,16},{24,28},{28,24},{32,36},... | collective-permute-start | bytes 933896 | tf_op jit(solution)/shard_map/ppermute | solution.py:330
  73.5 7.3 %collective-permute-start.6 = (s16[4,304,128]{2,1,0:T(8,128)(2,1)S(1)}, s16[4,304,128]{2,1,0:T(8,128)(2,1)S(1)}, u32[]{:S(2)}, u32[]{:S(2)}) collective-permute-start(s16[4,304,128]{2,1,0:T(8,128)(2,1)S(1)} %pad_add_fusion.refs_1_), channel_id=1, source_target_pairs={{0,8},{4,36},{8,16},{12,44},{16,24},{20,52},{24,0},{28,60},{32,40}... | collective-permute-start | bytes 933896 | tf_op jit(solution)/shard_map/ppermute | solution.py:331
  74.5 11.4 %collective-permute-start.5 = (s16[4,304,128]{2,1,0:T(8,128)(2,1)S(1)}, s16[4,304,128]{2,1,0:T(8,128)(2,1)S(1)}, u32[]{:S(2)}, u32[]{:S(2)}) collective-permute-start(s16[4,304,128]{2,1,0:T(8,128)(2,1)S(1)} %pad_add_fusion.refs_1_), channel_id=1, source_target_pairs={{0,24},{4,100},{8,0},{12,108},{16,8},{20,116},{24,16},{28,124},{32... | collective-permute-start | bytes 933896 | tf_op jit(solution)/shard_map/ppermute | solution.py:331
  79.0 8.2 %collective-permute-start.4 = (s16[4,304,128]{2,1,0:T(8,128)(2,1)S(1)}, s16[4,304,128]{2,1,0:T(8,128)(2,1)S(1)}, u32[]{:S(2)}, u32[]{:S(2)}) collective-permute-start(s16[4,304,128]{2,1,0:T(8,128)(2,1)S(1)} %pad_add_fusion.refs_1_), channel_id=1, source_target_pairs={{0,16},{4,68},{8,24},{12,76},{16,0},{20,84},{24,8},{28,92},{32,48}... | collective-permute-start | bytes 933896 | tf_op jit(solution)/shard_map/ppermute | solution.py:334
  80.8 7.3 %collective-permute-start.8 = (s16[4,304,128]{2,1,0:T(8,128)(2,1)S(1)}, s16[4,304,128]{2,1,0:T(8,128)(2,1)S(1)}, u32[]{:S(2)}, u32[]{:S(2)}) collective-permute-start(s16[4,304,128]{2,1,0:T(8,128)(2,1)S(1)} %collective-permute-done.6.refs_1_), channel_id=1, source_target_pairs={{0,4},{4,0},{8,12},{12,8},{16,20},{20,16},{24,28},{28,24},{32,36},... | collective-permute-start | bytes 933896 | tf_op jit(solution)/shard_map/ppermute | solution.py:337
  85.8 2.3 %collective-permute-start.9 = (s16[4,304,128]{2,1,0:T(8,128)(2,1)S(1)}, s16[4,304,128]{2,1,0:T(8,128)(2,1)S(1)}, u32[]{:S(2)}, u32[]{:S(2)}) collective-permute-start(s16[4,304,128]{2,1,0:T(8,128)(2,1)S(1)} %collective-permute-done.5.refs_1_), channel_id=1, source_target_pairs={{0,4},{4,0},{8,12},{12,8},{16,20},{20,16},{24,28},{28,24},{32,36},... | collective-permute-start | bytes 933896 | tf_op jit(solution)/shard_map/ppermute | solution.py:340
  87.1 2.7 %collective-permute-start.7 = (s16[4,304,128]{2,1,0:T(8,128)(2,1)S(1)}, s16[4,304,128]{2,1,0:T(8,128)(2,1)S(1)}, u32[]{:S(2)}, u32[]{:S(2)}) collective-permute-start(s16[4,304,128]{2,1,0:T(8,128)(2,1)S(1)} %collective-permute-done.4.refs_1_), channel_id=1, source_target_pairs={{0,4},{4,0},{8,12},{12,8},{16,20},{20,16},{24,28},{28,24},{32,36},... | collective-permute-start | bytes 933896 | tf_op jit(solution)/shard_map/ppermute | solution.py:343

commit v6 on v5

--- a/solution.py
+++ b/solution.py
@@ -329,20 +329,21 @@
     across = [(i, i ^ 1) for i in range(2 * SIDE * SIDE)]
     theirs = lax.ppermute(own, "wide", across)
     first, second = (lax.ppermute(own, "wide", along(1, shift)) for shift in (1, 3))
-    made = update([(0, 0), (1, 0)], me, [own, theirs], momentum, weights)
+    sibling = theirs
+    made = update([(0, 0)], me, [own], momentum, weights)
     again_own, *made = lax.optimization_barrier((own, *made))
     last = lax.ppermute(again_own, "wide", along(1, 2))
-    rest = [(0, 3), (1, 1), (1, 3), (0, 2), (1, 2)]
+    rest = [(1, 0), (0, 3), (1, 1), (1, 3), (0, 2), (1, 2)]
     first, *made = lax.optimization_barrier((first, *made))
     theirs = [lax.ppermute(first, "wide", across)]
     *made, given = update([(0, 1)], me, [first], momentum, weights, made, ahead=rest)
     second, *made = lax.optimization_barrier((second, *made))
     theirs = theirs + [lax.ppermute(second, "wide", across)]
-    made = update(rest[:1], me, [second], momentum, weights, made, given=given)
+    made = update(rest[:2], me, [sibling, second], momentum, weights, made, given=given)
     last, *made = lax.optimization_barrier((last, *made))
     theirs = theirs + [lax.ppermute(last, "wide", across)]
-    made = update(rest[1:3], me, theirs[:2], momentum, weights, made, given=given, first=1)
-    new_momentum, new_weights = update(rest[3:], me, [last, theirs[2]], momentum, weights, made, given=given, first=3)
+    made = update(rest[2:4], me, theirs[:2], momentum, weights, made, given=given, first=2)
+    new_momentum, new_weights = update(rest[4:], me, [last, theirs[2]], momentum, weights, made, given=given, first=4)
 
     def again(state):
         new_momentum = MOMENTUM_RATE * momentum + direct(x, counts)

time: 92.8 us -> 94.1 us (1.014)
  waiting for transfers between devices: 16.3 us -> 17.5 us
    ppermute x1, starting transfers between devices: 0.94 us -> 3.07 us  [shards(): theirs = [lax.ppermute(first, 'wide', across)]]
    ppermute x2, starting transfers between devices: 2.68 us -> 0.58 us  [shards(): lax.ppermute(own, 'wide', along(1, shift))]
    ppermute x1, starting transfers between devices: 1.47 us -> 3.03 us  [shards(): theirs = lax.ppermute(own, 'wide', across)]
    ppermute x3, waiting for transfers between devices: 3.48 us -> 4.75 us  [shards(): lax.ppermute(piece, 'wide', along(0, shift))]
    ppermute x3, starting transfers between devices: 2.74 us -> 1.6 us  [shards(): lax.ppermute(piece, 'wide', along(0, shift))]
  transfers between devices with their start and end apart: 11 -> 11, of which waited for: 4 -> 5; matrix products, arithmetic and copies ran while one was open for 0% -> 0% of each run, Pallas kernels for 11% -> 11%
where the time goes in v6:
time: 94.1 us; the launch traced here: 93.9 us
  blocking collectives  40.7 us (43%)
  waiting for transfers between devices  17.5 us (19%)
  Pallas kernels  16.2 us (17%)
  starting transfers between devices  15.4 us (16%)
  local copies, waits for them, and re-layouts  2.34 us (2%)
    all_to_all x1, blocking collectives, shards(): lax.all_to_all(pack(deltas, clients), 'wide', split_axis=0, concat_axis=0...  40.7 us
    all_to_all x1, waiting for transfers between devices, shards(): lax.all_to_all(gram_copies(x, devices), ('wide', 'narrow'), split_axis=0,...  12 us
    pallas_call x5, Pallas kernels, update(): pl.pallas_call(lambda *refs: update_kernel(parts, ahead, given is not Non...  11.9 us
    all_to_all x1, starting transfers between devices, shards(): lax.all_to_all(gram_copies(x, devices), ('wide', 'narrow'), split_axis=0,...  5.73 us
    ppermute x3, waiting for transfers between devices, shards(): lax.ppermute(piece, 'wide', along(0, shift))  4.75 us
    ppermute x1, starting transfers between devices, shards(): theirs = [lax.ppermute(first, 'wide', across)]  3.07 us
    ppermute x1, starting transfers between devices, shards(): theirs = lax.ppermute(own, 'wide', across)  3.03 us
    unnamed x4, local copies, waits for them, and re-layouts  2.34 us
  transfers between devices with their start and end apart: 11, of which 5 were waited for; matrix products, arithmetic and copies ran while one was open for 0% of the time, Pallas kernels for 11%

profile of v6, /device:TPU:1, one launch (start us, length us, event | category | flops | bytes accessed | tf_op | source)
XLA Modules:
  0.0 93.9 jit_solution(11184268213369784652)
XLA Ops:
  0.6 2.3 %copy-done = bf16[1,1179648]{1,0:T(2,128)(2,1)S(1)} copy-done((bf16[1,1179648]{1,0:T(2,128)(2,1)S(1)}, bf16[1,1179648]{1,0:T(2,128)(2,1)}, u32[]{:S(2)}) %copy-start) | copy-done | bytes 2359320
  3.0 0.3 shard_map.59
  3.3 0.0 copy-start.1
  3.3 40.7 %all_to_all.14.x_ref = bf16[32,288,128]{2,1,0:T(8,128)(2,1)S(1)} all-to-all(bf16[32,288,128]{2,1,0:T(8,128)(2,1)S(1)} %bitcast.13), channel_id=1, replica_groups=mesh['wide'=32,'narrow'=4] {'wide'}, dimensions={0} | all-to-all | bytes 4718592 | tf_op jit(solution)/shard_map/all_to_all | solution.py:318
  44.0 2.0 %shard_map.60 = f32[128,5,1,128]{3,2,1,0:T(1,128)} custom-call(bf16[32,288,128]{2,1,0:T(8,128)(2,1)S(1)} %all_to_all.14.x_ref), custom_call_target="tpu_custom_call" | custom-call | tf_op jit(solution)/shard_map/pallas_call | solution.py:75
  46.0 5.7 %all-to-all-start.2 = ((f32[128,5,1,128]{3,2,1,0:T(1,128)}), f32[128,5,1,128]{3,2,1,0:T(1,128)S(1)}, u32[]{:S(2)}, u32[]{:S(2)}) async-start(f32[128,5,1,128]{3,2,1,0:T(1,128)} %shard_map.60), calls=%async_computation.2 | async-start | bytes 655360 | tf_op jit(solution)/shard_map/all_to_all | solution.py:320
  51.8 12.0 %all-to-all-done.2.grams_ref = f32[128,5,1,128]{3,2,1,0:T(1,128)S(1)} async-done(((f32[128,5,1,128]{3,2,1,0:T(1,128)}), f32[128,5,1,128]{3,2,1,0:T(1,128)S(1)}, u32[]{:S(2)}, u32[]{:S(2)}) %all-to-all-start.2) | async-done | bytes 327712 | tf_op jit(solution)/shard_map/all_to_all | solution.py:320
  63.8 2.0 %shard_map.61 = (s16[304,128]{1,0:T(8,128)(2,1)S(1)}, s32[1]{0:T(128)}) custom-call(f32[128,5,1,128]{3,2,1,0:T(1,128)S(1)} %all-to-all-done.2.grams_ref, f32[1,128]{1,0:T(1,128)S(1)} %pad_bitcast_fusion.counts_ref, bf16[32,288,128]{2,1,0:T(8,128)(2,1)S(1)} %all_to_all.14.x_ref), custom_call_target="tpu_custom_call" | custom-call | tf_op jit(solution)/shard_map/pallas_call | solution.py:166
  65.8 0.5 collective-permute-start.2
  66.3 1.1 %collective-permute-start.1 = (s16[304,128]{1,0:T(8,128)(2,1)S(1)}, s16[304,128]{1,0:T(8,128)(2,1)S(1)}, u32[]{:S(2)}, u32[]{:S(2)}) collective-permute-start(s16[304,128]{1,0:T(8,128)(2,1)S(1)} %get-tuple-element.63), channel_id=1, source_target_pairs={{0,64},{4,20},{8,72},{12,28},{16,80},{20,4},{24,88},{28,12},{32,96... | collective-permute-start | bytes 233480 | tf_op jit(solution)/shard_map/ppermute | solution.py:326
  67.4 0.0 collective-permute-start
  67.4 2.0 %collective-permute-done.2 = s16[304,128]{1,0:T(8,128)(2,1)S(1)} collective-permute-done((s16[304,128]{1,0:T(8,128)(2,1)S(1)}, s16[304,128]{1,0:T(8,128)(2,1)S(1)}, u32[]{:S(2)}, u32[]{:S(2)}) %collective-permute-start.2) | collective-permute-done | bytes 77856 | tf_op jit(solution)/shard_map/ppermute | solution.py:326
  69.4 1.6 %collective-permute-done.1 = s16[304,128]{1,0:T(8,128)(2,1)S(1)} collective-permute-done((s16[304,128]{1,0:T(8,128)(2,1)S(1)}, s16[304,128]{1,0:T(8,128)(2,1)S(1)}, u32[]{:S(2)}, u32[]{:S(2)}) %collective-permute-start.1) | collective-permute-done | bytes 77856 | tf_op jit(solution)/shard_map/ppermute | solution.py:326
  71.0 1.1 %collective-permute-done = s16[304,128]{1,0:T(8,128)(2,1)S(1)} collective-permute-done((s16[304,128]{1,0:T(8,128)(2,1)S(1)}, s16[304,128]{1,0:T(8,128)(2,1)S(1)}, u32[]{:S(2)}, u32[]{:S(2)}) %collective-permute-start) | collective-permute-done | bytes 77856 | tf_op jit(solution)/shard_map/ppermute | solution.py:326
  72.2 0.1 collective-permute-start.6
  72.3 3.0 %collective-permute-start.4 = (s16[4,304,128]{2,1,0:T(8,128)(2,1)S(1)}, s16[4,304,128]{2,1,0:T(8,128)(2,1)S(1)}, u32[]{:S(2)}, u32[]{:S(2)}) collective-permute-start(s16[4,304,128]{2,1,0:T(8,128)(2,1)S(1)} %pad_add_fusion.refs_1_), channel_id=1, source_target_pairs={{0,4},{4,0},{8,12},{12,8},{16,20},{20,16},{24,28},{28,24},{32,36},... | collective-permute-start | bytes 933896 | tf_op jit(solution)/shard_map/ppermute | solution.py:330
  75.3 0.5 collective-permute-start.5
  75.8 2.2 %shard_map.62 = (f32[32,288,128]{2,1,0:T(8,128)}, f32[32,288,128]{2,1,0:T(8,128)}) custom-call(s32[1]{0:T(128)} %bitcast.3.refs_0_, s16[4,304,128]{2,1,0:T(8,128)(2,1)S(1)} %pad_add_fusion.refs_1_, f32[32,288,128]{2,1,0:T(8,128)} %bitcast.15, f32[32,288,128]{2,1,0:T(8,128)} %bitcast.21), custom_call_target="tpu_custom_call" | custom-call | flops 1 | bytes 1 | tf_op jit(solution)/shard_map/pallas_call | solution.py:270
  78.0 0.7 collective-permute-start.3
  78.8 0.8 collective-permute-done.6.refs_1_
  79.5 3.1 %collective-permute-start.8 = (s16[4,304,128]{2,1,0:T(8,128)(2,1)S(1)}, s16[4,304,128]{2,1,0:T(8,128)(2,1)S(1)}, u32[]{:S(2)}, u32[]{:S(2)}) collective-permute-start(s16[4,304,128]{2,1,0:T(8,128)(2,1)S(1)} %collective-permute-done.6.refs_1_), channel_id=1, source_target_pairs={{0,4},{4,0},{8,12},{12,8},{16,20},{20,16},{24,28},{28,24},{32,36},... | collective-permute-start | bytes 933896 | tf_op jit(solution)/shard_map/ppermute | solution.py:338
  82.6 4.5 %shard_map.63 = (f32[32,288,128]{2,1,0:T(8,128)}, f32[32,288,128]{2,1,0:T(8,128)}, f32[24,2,288,128]{3,2,1,0:T(8,128)S(1)}) custom-call(s32[1]{0:T(128)} %bitcast.3.refs_0_, s16[4,304,128]{2,1,0:T(8,128)(2,1)S(1)} %collective-permute-done.6.refs_1_, f32[32,288,128]{2,1,0:T(8,128)} %bitcast.16, ...), custom_call_target="tpu_custom_call", output_to_operand_aliasing={{0}: (4, {}), {1}: (5, {})} | custom-call | flops 1 | bytes 1 | tf_op jit(solution)/shard_map/pallas_call | solution.py:270
  87.1 0.0 collective-permute-done.5.refs_2_
  87.1 0.1 collective-permute-start.9
  87.2 0.0 collective-permute-done.4.refs_1_
  87.2 1.7 %shard_map.64 = (f32[32,288,128]{2,1,0:T(8,128)}, f32[32,288,128]{2,1,0:T(8,128)}) custom-call(s32[1]{0:T(128)} %bitcast.3.refs_0_, s16[4,304,128]{2,1,0:T(8,128)(2,1)S(1)} %collective-permute-done.4.refs_1_, s16[4,304,128]{2,1,0:T(8,128)(2,1)S(1)} %collective-permute-done.5.refs_2_, ...), custom_call_target="tpu_custom_call", output_to_operand_aliasing={{0}: (5, {}), {1}: (6, {})} | custom-call | flops 1 | bytes 1 | tf_op jit(solution)/shard_map/pallas_call | solution.py:270
  88.9 0.0 collective-permute-done.3.refs_1_
  88.9 0.6 collective-permute-start.7
  89.5 0.0 collective-permute-done.9.refs_2_
  89.5 1.7 %shard_map.65 = (f32[32,288,128]{2,1,0:T(8,128)}, f32[32,288,128]{2,1,0:T(8,128)}) custom-call(s32[1]{0:T(128)} %bitcast.3.refs_0_, s16[4,304,128]{2,1,0:T(8,128)(2,1)S(1)} %collective-permute-done.8.refs_1_, s16[4,304,128]{2,1,0:T(8,128)(2,1)S(1)} %collective-permute-done.9.refs_2_, ...), custom_call_target="tpu_custom_call", output_to_operand_aliasing={{0}: (5, {}), {1}: (6, {})} | custom-call | flops 1 | bytes 1 | tf_op jit(solution)/shard_map/pallas_call | solution.py:270
  91.2 1.7 %shard_map.66 = (f32[32,288,128]{2,1,0:T(8,128)}, f32[32,288,128]{2,1,0:T(8,128)}) custom-call(s32[1]{0:T(128)} %bitcast.3.refs_0_, s16[4,304,128]{2,1,0:T(8,128)(2,1)S(1)} %collective-permute-done.3.refs_1_, s16[4,304,128]{2,1,0:T(8,128)(2,1)S(1)} %collective-permute-done.7.refs_2_, ...), custom_call_target="tpu_custom_call", output_to_operand_aliasing={{0}: (5, {}), {1}: (6, {})} | custom-call | flops 1 | bytes 1 | tf_op jit(solution)/shard_map/pallas_call | solution.py:270
  93.0 0.7 while.11
  (7 shorter events, 0.1 us)
Async XLA Ops:
  0.6 2.3 %copy-start = (bf16[1,1179648]{1,0:T(2,128)(2,1)S(1)}, bf16[1,1179648]{1,0:T(2,128)(2,1)}, u32[]{:S(2)}) copy-start(bf16[1,1179648]{1,0:T(2,128)(2,1)} %flat_ref.1) | copy-start | bytes 7077892
  3.3 48.4 %copy-start.1 = (s32[32]{0:T(128)S(1)}, s32[32]{0:T(128)}, u32[]{:S(2)}) copy-start(s32[32]{0:T(128)} %param.7) | copy-start | bytes 388
  46.0 17.8 %all-to-all-start.2 = ((f32[128,5,1,128]{3,2,1,0:T(1,128)}), f32[128,5,1,128]{3,2,1,0:T(1,128)S(1)}, u32[]{:S(2)}, u32[]{:S(2)}) async-start(f32[128,5,1,128]{3,2,1,0:T(1,128)} %shard_map.60), calls=%async_computation.2 | async-start | bytes 655360 | tf_op jit(solution)/shard_map/all_to_all | solution.py:320
  65.8 3.6 %collective-permute-start.2 = (s16[304,128]{1,0:T(8,128)(2,1)S(1)}, s16[304,128]{1,0:T(8,128)(2,1)S(1)}, u32[]{:S(2)}, u32[]{:S(2)}) collective-permute-start(s16[304,128]{1,0:T(8,128)(2,1)S(1)} %get-tuple-element.63), channel_id=1, source_target_pairs={{0,96},{4,28},{8,104},{12,4},{16,112},{20,12},{24,120},{28,20},{32... | collective-permute-start | bytes 233480 | tf_op jit(solution)/shard_map/ppermute | solution.py:326
  66.3 4.8 %collective-permute-start.1 = (s16[304,128]{1,0:T(8,128)(2,1)S(1)}, s16[304,128]{1,0:T(8,128)(2,1)S(1)}, u32[]{:S(2)}, u32[]{:S(2)}) collective-permute-start(s16[304,128]{1,0:T(8,128)(2,1)S(1)} %get-tuple-element.63), channel_id=1, source_target_pairs={{0,64},{4,20},{8,72},{12,28},{16,80},{20,4},{24,88},{28,12},{32,96... | collective-permute-start | bytes 233480 | tf_op jit(solution)/shard_map/ppermute | solution.py:326
  67.4 4.8 %collective-permute-start = (s16[304,128]{1,0:T(8,128)(2,1)S(1)}, s16[304,128]{1,0:T(8,128)(2,1)S(1)}, u32[]{:S(2)}, u32[]{:S(2)}) collective-permute-start(s16[304,128]{1,0:T(8,128)(2,1)S(1)} %get-tuple-element.63), channel_id=1, source_target_pairs={{0,32},{4,12},{8,40},{12,20},{16,48},{20,28},{24,56},{28,4},{32,64... | collective-permute-start | bytes 233480 | tf_op jit(solution)/shard_map/ppermute | solution.py:326
  72.2 7.3 %collective-permute-start.6 = (s16[4,304,128]{2,1,0:T(8,128)(2,1)S(1)}, s16[4,304,128]{2,1,0:T(8,128)(2,1)S(1)}, u32[]{:S(2)}, u32[]{:S(2)}) collective-permute-start(s16[4,304,128]{2,1,0:T(8,128)(2,1)S(1)} %pad_add_fusion.refs_1_), channel_id=1, source_target_pairs={{0,8},{4,36},{8,16},{12,44},{16,24},{20,52},{24,0},{28,60},{32,40}... | collective-permute-start | bytes 933896 | tf_op jit(solution)/shard_map/ppermute | solution.py:331
  72.3 14.9 %collective-permute-start.4 = (s16[4,304,128]{2,1,0:T(8,128)(2,1)S(1)}, s16[4,304,128]{2,1,0:T(8,128)(2,1)S(1)}, u32[]{:S(2)}, u32[]{:S(2)}) collective-permute-start(s16[4,304,128]{2,1,0:T(8,128)(2,1)S(1)} %pad_add_fusion.refs_1_), channel_id=1, source_target_pairs={{0,4},{4,0},{8,12},{12,8},{16,20},{20,16},{24,28},{28,24},{32,36},... | collective-permute-start | bytes 933896 | tf_op jit(solution)/shard_map/ppermute | solution.py:330
  75.3 11.8 %collective-permute-start.5 = (s16[4,304,128]{2,1,0:T(8,128)(2,1)S(1)}, s16[4,304,128]{2,1,0:T(8,128)(2,1)S(1)}, u32[]{:S(2)}, u32[]{:S(2)}) collective-permute-start(s16[4,304,128]{2,1,0:T(8,128)(2,1)S(1)} %pad_add_fusion.refs_1_), channel_id=1, source_target_pairs={{0,24},{4,100},{8,0},{12,108},{16,8},{20,116},{24,16},{28,124},{32... | collective-permute-start | bytes 933896 | tf_op jit(solution)/shard_map/ppermute | solution.py:331
  78.0 10.9 %collective-permute-start.3 = (s16[4,304,128]{2,1,0:T(8,128)(2,1)S(1)}, s16[4,304,128]{2,1,0:T(8,128)(2,1)S(1)}, u32[]{:S(2)}, u32[]{:S(2)}) collective-permute-start(s16[4,304,128]{2,1,0:T(8,128)(2,1)S(1)} %pad_add_fusion.refs_1_), channel_id=1, source_target_pairs={{0,16},{4,68},{8,24},{12,76},{16,0},{20,84},{24,8},{28,92},{32,48}... | collective-permute-start | bytes 933896 | tf_op jit(solution)/shard_map/ppermute | solution.py:335
  79.5 10.0 %collective-permute-start.8 = (s16[4,304,128]{2,1,0:T(8,128)(2,1)S(1)}, s16[4,304,128]{2,1,0:T(8,128)(2,1)S(1)}, u32[]{:S(2)}, u32[]{:S(2)}) collective-permute-start(s16[4,304,128]{2,1,0:T(8,128)(2,1)S(1)} %collective-permute-done.6.refs_1_), channel_id=1, source_target_pairs={{0,4},{4,0},{8,12},{12,8},{16,20},{20,16},{24,28},{28,24},{32,36},... | collective-permute-start | bytes 933896 | tf_op jit(solution)/shard_map/ppermute | solution.py:338
  87.1 2.4 %collective-permute-start.9 = (s16[4,304,128]{2,1,0:T(8,128)(2,1)S(1)}, s16[4,304,128]{2,1,0:T(8,128)(2,1)S(1)}, u32[]{:S(2)}, u32[]{:S(2)}) collective-permute-start(s16[4,304,128]{2,1,0:T(8,128)(2,1)S(1)} %collective-permute-done.5.refs_2_), channel_id=1, source_target_pairs={{0,4},{4,0},{8,12},{12,8},{16,20},{20,16},{24,28},{28,24},{32,36},... | collective-permute-start | bytes 933896 | tf_op jit(solution)/shard_map/ppermute | solution.py:341
  88.9 2.3 %collective-permute-start.7 = (s16[4,304,128]{2,1,0:T(8,128)(2,1)S(1)}, s16[4,304,128]{2,1,0:T(8,128)(2,1)S(1)}, u32[]{:S(2)}, u32[]{:S(2)}) collective-permute-start(s16[4,304,128]{2,1,0:T(8,128)(2,1)S(1)} %collective-permute-done.3.refs_1_), channel_id=1, source_target_pairs={{0,4},{4,0},{8,12},{12,8},{16,20},{20,16},{24,28},{28,24},{32,36},... | collective-permute-start | bytes 933896 | tf_op jit(solution)/shard_map/ppermute | solution.py:344

commit v7 on v5

--- a/solution.py
+++ b/solution.py
@@ -28,22 +28,31 @@
     return pltpu.CompilerParams(vmem_limit_bytes=VMEM, **more)
 
 
-def pack_kernel(flat_ref, packed_ref):
-    packed_ref[...] = flat_ref[...].reshape(packed_ref.shape)
+def pack_kernel(flat_ref, packed_ref, held, sem):
+    parts = sem.shape[0]
+    entries, rows = flat_ref.shape[1] // parts, packed_ref.shape[0] // parts
+
+    def fetch(i):
+        at = pl.ds(i * entries, entries)
+        return pltpu.make_async_copy(flat_ref.at[:, at], held.at[:, at], sem.at[i])
+
+    for i in range(parts):
+        fetch(i).start()
+    for i in range(parts):
+        fetch(i).wait()
+        packed_ref[i * rows : (i + 1) * rows, :] = held[:, i * entries : (i + 1) * entries].reshape(rows, LANES)
 
 
 def pack(deltas, clients):
-    entries = deltas.shape[1]
-    rows = entries // LANES
-    steps = 2
+    rows = deltas.shape[1] // LANES
     packed = pl.pallas_call(
         pack_kernel,
-        grid=(steps,),
-        in_specs=[pl.BlockSpec((1, entries // steps), lambda i: (0, i))],
-        out_specs=pl.BlockSpec((rows // steps, LANES), lambda i: (i, 0)),
-        out_shape=jax.ShapeDtypeStruct((rows, LANES), deltas.dtype),
+        in_specs=[pl.BlockSpec(memory_space=pltpu.HBM)],
+        out_specs=pl.BlockSpec(memory_space=pltpu.VMEM),
+        out_shape=pltpu.VMEM((rows, LANES), deltas.dtype),
+        scratch_shapes=[pltpu.VMEM(deltas.shape, deltas.dtype), pltpu.SemaphoreType.DMA((8,))],
         compiler_params=params(),
-    )(deltas)
+    )(pltpu.with_memory_space_constraint(deltas, pltpu.HBM))
     return packed.reshape(clients, rows // clients, LANES)
 
 

time: 92.8 us -> 92.5 us (level)
  local copies, waits for them, and re-layouts: 2.34 us -> 0.01 us
  Pallas kernels: 15.8 us -> 17.9 us
    unnamed x4 -> x2, local copies, waits for them, and re-layouts: 2.34 us -> 0.01 us
    pallas_call x1, Pallas kernels: 0.33 us -> 2.42 us  [pack(): pl.pallas_call(pack_kernel, in_specs=[pl.BlockSpec(memory_space=pltpu.HBM...]
where the time goes in v7:
time: 92.5 us; the launch traced here: 92.2 us
  blocking collectives  40.7 us (44%)
  Pallas kernels  17.9 us (19%)
  waiting for transfers between devices  16.3 us (18%)
  starting transfers between devices  15.6 us (17%)
  between operations  0.93 us (1%)
    all_to_all x1, blocking collectives, shards(): lax.all_to_all(pack(deltas, clients), 'wide', split_axis=0, concat_axis=0...  40.7 us
    all_to_all x1, waiting for transfers between devices, shards(): lax.all_to_all(gram_copies(x, devices), ('wide', 'narrow'), split_axis=0,...  12 us
    pallas_call x5, Pallas kernels, update(): pl.pallas_call(lambda *refs: update_kernel(parts, ahead, given is not Non...  11.5 us
    all_to_all x1, starting transfers between devices, shards(): lax.all_to_all(gram_copies(x, devices), ('wide', 'narrow'), split_axis=0,...  5.73 us
    ppermute x3, waiting for transfers between devices, shards(): lax.ppermute(piece, 'wide', along(0, shift))  3.48 us
    ppermute x3, starting transfers between devices, shards(): lax.ppermute(piece, 'wide', along(0, shift))  2.74 us
    ppermute x2, starting transfers between devices, shards(): lax.ppermute(own, 'wide', along(1, shift))  2.68 us
    pallas_call x1, Pallas kernels, pack(): pl.pallas_call(pack_kernel, in_specs=[pl.BlockSpec(memory_space=pltpu.HBM...  2.42 us
  transfers between devices with their start and end apart: 11, of which 4 were waited for; matrix products, arithmetic and copies ran while one was open for 0% of the time, Pallas kernels for 11%

profile of v7, /device:TPU:1, one launch (start us, length us, event | category | flops | bytes accessed | tf_op | source)
XLA Modules:
  0.0 92.2 jit_solution(1614914694864528183)
XLA Ops:
  0.6 2.4 %shard_map.59 = bf16[9216,128]{1,0:T(8,128)(2,1)S(1)} custom-call(bf16[1,1179648]{1,0:T(2,128)(2,1)} %flat_ref.1), custom_call_target="tpu_custom_call" | custom-call | tf_op jit(solution)/shard_map/pallas_call | solution.py:48
  3.1 0.0 copy-start
  3.1 40.7 %all_to_all.14.x_ref = bf16[32,288,128]{2,1,0:T(8,128)(2,1)S(1)} all-to-all(bf16[32,288,128]{2,1,0:T(8,128)(2,1)S(1)} %bitcast.13), channel_id=1, replica_groups=mesh['wide'=32,'narrow'=4] {'wide'}, dimensions={0} | all-to-all | bytes 4718592 | tf_op jit(solution)/shard_map/all_to_all | solution.py:327
  43.8 2.0 %shard_map.60 = f32[128,5,1,128]{3,2,1,0:T(1,128)} custom-call(bf16[32,288,128]{2,1,0:T(8,128)(2,1)S(1)} %all_to_all.14.x_ref), custom_call_target="tpu_custom_call" | custom-call | tf_op jit(solution)/shard_map/pallas_call | solution.py:84
  45.8 5.7 %all-to-all-start.2 = ((f32[128,5,1,128]{3,2,1,0:T(1,128)}), f32[128,5,1,128]{3,2,1,0:T(1,128)S(1)}, u32[]{:S(2)}, u32[]{:S(2)}) async-start(f32[128,5,1,128]{3,2,1,0:T(1,128)} %shard_map.60), calls=%async_computation.2 | async-start | bytes 655360 | tf_op jit(solution)/shard_map/all_to_all | solution.py:329
  51.5 12.0 %all-to-all-done.2.grams_ref = f32[128,5,1,128]{3,2,1,0:T(1,128)S(1)} async-done(((f32[128,5,1,128]{3,2,1,0:T(1,128)}), f32[128,5,1,128]{3,2,1,0:T(1,128)S(1)}, u32[]{:S(2)}, u32[]{:S(2)}) %all-to-all-start.2) | async-done | bytes 327712 | tf_op jit(solution)/shard_map/all_to_all | solution.py:329
  63.5 2.0 %shard_map.61 = (s16[304,128]{1,0:T(8,128)(2,1)S(1)}, s32[1]{0:T(128)}) custom-call(f32[128,5,1,128]{3,2,1,0:T(1,128)S(1)} %all-to-all-done.2.grams_ref, f32[1,128]{1,0:T(1,128)S(1)} %pad_bitcast_fusion.counts_ref, bf16[32,288,128]{2,1,0:T(8,128)(2,1)S(1)} %all_to_all.14.x_ref), custom_call_target="tpu_custom_call" | custom-call | tf_op jit(solution)/shard_map/pallas_call | solution.py:175
  65.5 0.1 collective-permute-start
  65.6 1.6 %collective-permute-start.1 = (s16[304,128]{1,0:T(8,128)(2,1)S(1)}, s16[304,128]{1,0:T(8,128)(2,1)S(1)}, u32[]{:S(2)}, u32[]{:S(2)}) collective-permute-start(s16[304,128]{1,0:T(8,128)(2,1)S(1)} %get-tuple-element.63), channel_id=1, source_target_pairs={{0,64},{4,20},{8,72},{12,28},{16,80},{20,4},{24,88},{28,12},{32,96... | collective-permute-start | bytes 233480 | tf_op jit(solution)/shard_map/ppermute | solution.py:335
  67.2 1.1 %collective-permute-start.2 = (s16[304,128]{1,0:T(8,128)(2,1)S(1)}, s16[304,128]{1,0:T(8,128)(2,1)S(1)}, u32[]{:S(2)}, u32[]{:S(2)}) collective-permute-start(s16[304,128]{1,0:T(8,128)(2,1)S(1)} %get-tuple-element.63), channel_id=1, source_target_pairs={{0,96},{4,28},{8,104},{12,4},{16,112},{20,12},{24,120},{28,20},{32... | collective-permute-start | bytes 233480 | tf_op jit(solution)/shard_map/ppermute | solution.py:335
  68.3 2.9 %collective-permute-done = s16[304,128]{1,0:T(8,128)(2,1)S(1)} collective-permute-done((s16[304,128]{1,0:T(8,128)(2,1)S(1)}, s16[304,128]{1,0:T(8,128)(2,1)S(1)}, u32[]{:S(2)}, u32[]{:S(2)}) %collective-permute-start) | collective-permute-done | bytes 77856 | tf_op jit(solution)/shard_map/ppermute | solution.py:335
  71.2 0.0 collective-permute-done.1
  71.2 0.6 collective-permute-done.2
  71.8 1.5 %collective-permute-start.3 = (s16[4,304,128]{2,1,0:T(8,128)(2,1)S(1)}, s16[4,304,128]{2,1,0:T(8,128)(2,1)S(1)}, u32[]{:S(2)}, u32[]{:S(2)}) collective-permute-start(s16[4,304,128]{2,1,0:T(8,128)(2,1)S(1)} %pad_add_fusion.refs_1_), channel_id=1, source_target_pairs={{0,4},{4,0},{8,12},{12,8},{16,20},{20,16},{24,28},{28,24},{32,36},... | collective-permute-start | bytes 933896 | tf_op jit(solution)/shard_map/ppermute | solution.py:339
  73.3 0.9 collective-permute-start.6
  74.2 1.8 %collective-permute-start.5 = (s16[4,304,128]{2,1,0:T(8,128)(2,1)S(1)}, s16[4,304,128]{2,1,0:T(8,128)(2,1)S(1)}, u32[]{:S(2)}, u32[]{:S(2)}) collective-permute-start(s16[4,304,128]{2,1,0:T(8,128)(2,1)S(1)} %pad_add_fusion.refs_1_), channel_id=1, source_target_pairs={{0,24},{4,100},{8,0},{12,108},{16,8},{20,116},{24,16},{28,124},{32... | collective-permute-start | bytes 933896 | tf_op jit(solution)/shard_map/ppermute | solution.py:340
  76.0 0.0 collective-permute-done.3.refs_2_
  76.0 2.8 %shard_map.62 = (f32[32,288,128]{2,1,0:T(8,128)}, f32[32,288,128]{2,1,0:T(8,128)}) custom-call(s32[1]{0:T(128)} %bitcast.3.refs_0_, s16[4,304,128]{2,1,0:T(8,128)(2,1)S(1)} %pad_add_fusion.refs_1_, s16[4,304,128]{2,1,0:T(8,128)(2,1)S(1)} %collective-permute-done.3.refs_2_, f32[32,288,128]{2,1,0:T(8,128)} %bitcast.15, f32[32,288,128]{2,1,0:T(8,128)} %bitcast.21), custom_call_target="tpu_custom_call" | custom-call | flops 1 | bytes 1 | tf_op jit(solution)/shard_map/pallas_call | solution.py:279
  78.7 1.0 %collective-permute-start.4 = (s16[4,304,128]{2,1,0:T(8,128)(2,1)S(1)}, s16[4,304,128]{2,1,0:T(8,128)(2,1)S(1)}, u32[]{:S(2)}, u32[]{:S(2)}) collective-permute-start(s16[4,304,128]{2,1,0:T(8,128)(2,1)S(1)} %pad_add_fusion.refs_1_), channel_id=1, source_target_pairs={{0,16},{4,68},{8,24},{12,76},{16,0},{20,84},{24,8},{28,92},{32,48}... | collective-permute-start | bytes 933896 | tf_op jit(solution)/shard_map/ppermute | solution.py:343
  79.7 0.8 collective-permute-done.6.refs_1_
  80.5 0.9 %collective-permute-start.8 = (s16[4,304,128]{2,1,0:T(8,128)(2,1)S(1)}, s16[4,304,128]{2,1,0:T(8,128)(2,1)S(1)}, u32[]{:S(2)}, u32[]{:S(2)}) collective-permute-start(s16[4,304,128]{2,1,0:T(8,128)(2,1)S(1)} %collective-permute-done.6.refs_1_), channel_id=1, source_target_pairs={{0,4},{4,0},{8,12},{12,8},{16,20},{20,16},{24,28},{28,24},{32,36},... | collective-permute-start | bytes 933896 | tf_op jit(solution)/shard_map/ppermute | solution.py:346
  81.5 4.1 %shard_map.63 = (f32[32,288,128]{2,1,0:T(8,128)}, f32[32,288,128]{2,1,0:T(8,128)}, f32[20,2,288,128]{3,2,1,0:T(8,128)S(1)}) custom-call(s32[1]{0:T(128)} %bitcast.3.refs_0_, s16[4,304,128]{2,1,0:T(8,128)(2,1)S(1)} %collective-permute-done.6.refs_1_, f32[32,288,128]{2,1,0:T(8,128)} %bitcast.16, ...), custom_call_target="tpu_custom_call", output_to_operand_aliasing={{0}: (4, {}), {1}: (5, {})} | custom-call | flops 1 | bytes 1 | tf_op jit(solution)/shard_map/pallas_call | solution.py:279
  85.6 0.0 collective-permute-done.5.refs_1_
  85.6 0.1 collective-permute-start.9
  85.7 1.2 %shard_map.64 = (f32[32,288,128]{2,1,0:T(8,128)}, f32[32,288,128]{2,1,0:T(8,128)}) custom-call(s32[1]{0:T(128)} %bitcast.3.refs_0_, s16[4,304,128]{2,1,0:T(8,128)(2,1)S(1)} %collective-permute-done.5.refs_1_, f32[32,288,128]{2,1,0:T(8,128)} %bitcast.17, f32[32,288,128]{2,1,0:T(8,128)} %bitcast.23, ...), custom_call_target="tpu_custom_call", output_to_operand_aliasing={{0}: (4, {}), {1}: (5, {})} | custom-call | flops 1 | bytes 1 | tf_op jit(solution)/shard_map/pallas_call | solution.py:279
  86.9 0.0 collective-permute-done.4.refs_1_
  86.9 1.0 %collective-permute-start.7 = (s16[4,304,128]{2,1,0:T(8,128)(2,1)S(1)}, s16[4,304,128]{2,1,0:T(8,128)(2,1)S(1)}, u32[]{:S(2)}, u32[]{:S(2)}) collective-permute-start(s16[4,304,128]{2,1,0:T(8,128)(2,1)S(1)} %collective-permute-done.4.refs_1_), channel_id=1, source_target_pairs={{0,4},{4,0},{8,12},{12,8},{16,20},{20,16},{24,28},{28,24},{32,36},... | collective-permute-start | bytes 933896 | tf_op jit(solution)/shard_map/ppermute | solution.py:352
  87.9 0.0 collective-permute-done.9.refs_2_
  87.9 0.0 collective-permute-done.8.refs_1_
  87.9 1.7 %shard_map.65 = (f32[32,288,128]{2,1,0:T(8,128)}, f32[32,288,128]{2,1,0:T(8,128)}) custom-call(s32[1]{0:T(128)} %bitcast.3.refs_0_, s16[4,304,128]{2,1,0:T(8,128)(2,1)S(1)} %collective-permute-done.8.refs_1_, s16[4,304,128]{2,1,0:T(8,128)(2,1)S(1)} %collective-permute-done.9.refs_2_, ...), custom_call_target="tpu_custom_call", output_to_operand_aliasing={{0}: (5, {}), {1}: (6, {})} | custom-call | flops 1 | bytes 1 | tf_op jit(solution)/shard_map/pallas_call | solution.py:279
  89.6 1.7 %shard_map.66 = (f32[32,288,128]{2,1,0:T(8,128)}, f32[32,288,128]{2,1,0:T(8,128)}) custom-call(s32[1]{0:T(128)} %bitcast.3.refs_0_, s16[4,304,128]{2,1,0:T(8,128)(2,1)S(1)} %collective-permute-done.4.refs_1_, s16[4,304,128]{2,1,0:T(8,128)(2,1)S(1)} %collective-permute-done.7.refs_2_, ...), custom_call_target="tpu_custom_call", output_to_operand_aliasing={{0}: (5, {}), {1}: (6, {})} | custom-call | flops 1 | bytes 1 | tf_op jit(solution)/shard_map/pallas_call | solution.py:279
  91.3 0.7 while.11
  (5 shorter events, 0.0 us)
Async XLA Ops:
  3.1 48.4 %copy-start = (s32[32]{0:T(128)S(1)}, s32[32]{0:T(128)}, u32[]{:S(2)}) copy-start(s32[32]{0:T(128)} %param.7) | copy-start | bytes 388
  45.8 17.8 %all-to-all-start.2 = ((f32[128,5,1,128]{3,2,1,0:T(1,128)}), f32[128,5,1,128]{3,2,1,0:T(1,128)S(1)}, u32[]{:S(2)}, u32[]{:S(2)}) async-start(f32[128,5,1,128]{3,2,1,0:T(1,128)} %shard_map.60), calls=%async_computation.2 | async-start | bytes 655360 | tf_op jit(solution)/shard_map/all_to_all | solution.py:329
  65.5 5.7 %collective-permute-start = (s16[304,128]{1,0:T(8,128)(2,1)S(1)}, s16[304,128]{1,0:T(8,128)(2,1)S(1)}, u32[]{:S(2)}, u32[]{:S(2)}) collective-permute-start(s16[304,128]{1,0:T(8,128)(2,1)S(1)} %get-tuple-element.63), channel_id=1, source_target_pairs={{0,32},{4,12},{8,40},{12,20},{16,48},{20,28},{24,56},{28,4},{32,64... | collective-permute-start | bytes 233480 | tf_op jit(solution)/shard_map/ppermute | solution.py:335
  65.6 5.6 %collective-permute-start.1 = (s16[304,128]{1,0:T(8,128)(2,1)S(1)}, s16[304,128]{1,0:T(8,128)(2,1)S(1)}, u32[]{:S(2)}, u32[]{:S(2)}) collective-permute-start(s16[304,128]{1,0:T(8,128)(2,1)S(1)} %get-tuple-element.63), channel_id=1, source_target_pairs={{0,64},{4,20},{8,72},{12,28},{16,80},{20,4},{24,88},{28,12},{32,96... | collective-permute-start | bytes 233480 | tf_op jit(solution)/shard_map/ppermute | solution.py:335
  67.2 4.6 %collective-permute-start.2 = (s16[304,128]{1,0:T(8,128)(2,1)S(1)}, s16[304,128]{1,0:T(8,128)(2,1)S(1)}, u32[]{:S(2)}, u32[]{:S(2)}) collective-permute-start(s16[304,128]{1,0:T(8,128)(2,1)S(1)} %get-tuple-element.63), channel_id=1, source_target_pairs={{0,96},{4,28},{8,104},{12,4},{16,112},{20,12},{24,120},{28,20},{32... | collective-permute-start | bytes 233480 | tf_op jit(solution)/shard_map/ppermute | solution.py:335
  71.8 4.2 %collective-permute-start.3 = (s16[4,304,128]{2,1,0:T(8,128)(2,1)S(1)}, s16[4,304,128]{2,1,0:T(8,128)(2,1)S(1)}, u32[]{:S(2)}, u32[]{:S(2)}) collective-permute-start(s16[4,304,128]{2,1,0:T(8,128)(2,1)S(1)} %pad_add_fusion.refs_1_), channel_id=1, source_target_pairs={{0,4},{4,0},{8,12},{12,8},{16,20},{20,16},{24,28},{28,24},{32,36},... | collective-permute-start | bytes 933896 | tf_op jit(solution)/shard_map/ppermute | solution.py:339
  73.3 7.3 %collective-permute-start.6 = (s16[4,304,128]{2,1,0:T(8,128)(2,1)S(1)}, s16[4,304,128]{2,1,0:T(8,128)(2,1)S(1)}, u32[]{:S(2)}, u32[]{:S(2)}) collective-permute-start(s16[4,304,128]{2,1,0:T(8,128)(2,1)S(1)} %pad_add_fusion.refs_1_), channel_id=1, source_target_pairs={{0,8},{4,36},{8,16},{12,44},{16,24},{20,52},{24,0},{28,60},{32,40}... | collective-permute-start | bytes 933896 | tf_op jit(solution)/shard_map/ppermute | solution.py:340
  74.2 11.4 %collective-permute-start.5 = (s16[4,304,128]{2,1,0:T(8,128)(2,1)S(1)}, s16[4,304,128]{2,1,0:T(8,128)(2,1)S(1)}, u32[]{:S(2)}, u32[]{:S(2)}) collective-permute-start(s16[4,304,128]{2,1,0:T(8,128)(2,1)S(1)} %pad_add_fusion.refs_1_), channel_id=1, source_target_pairs={{0,24},{4,100},{8,0},{12,108},{16,8},{20,116},{24,16},{28,124},{32... | collective-permute-start | bytes 933896 | tf_op jit(solution)/shard_map/ppermute | solution.py:340
  78.7 8.2 %collective-permute-start.4 = (s16[4,304,128]{2,1,0:T(8,128)(2,1)S(1)}, s16[4,304,128]{2,1,0:T(8,128)(2,1)S(1)}, u32[]{:S(2)}, u32[]{:S(2)}) collective-permute-start(s16[4,304,128]{2,1,0:T(8,128)(2,1)S(1)} %pad_add_fusion.refs_1_), channel_id=1, source_target_pairs={{0,16},{4,68},{8,24},{12,76},{16,0},{20,84},{24,8},{28,92},{32,48}... | collective-permute-start | bytes 933896 | tf_op jit(solution)/shard_map/ppermute | solution.py:343
  80.5 7.3 %collective-permute-start.8 = (s16[4,304,128]{2,1,0:T(8,128)(2,1)S(1)}, s16[4,304,128]{2,1,0:T(8,128)(2,1)S(1)}, u32[]{:S(2)}, u32[]{:S(2)}) collective-permute-start(s16[4,304,128]{2,1,0:T(8,128)(2,1)S(1)} %collective-permute-done.6.refs_1_), channel_id=1, source_target_pairs={{0,4},{4,0},{8,12},{12,8},{16,20},{20,16},{24,28},{28,24},{32,36},... | collective-permute-start | bytes 933896 | tf_op jit(solution)/shard_map/ppermute | solution.py:346
  85.6 2.3 %collective-permute-start.9 = (s16[4,304,128]{2,1,0:T(8,128)(2,1)S(1)}, s16[4,304,128]{2,1,0:T(8,128)(2,1)S(1)}, u32[]{:S(2)}, u32[]{:S(2)}) collective-permute-start(s16[4,304,128]{2,1,0:T(8,128)(2,1)S(1)} %collective-permute-done.5.refs_1_), channel_id=1, source_target_pairs={{0,4},{4,0},{8,12},{12,8},{16,20},{20,16},{24,28},{28,24},{32,36},... | collective-permute-start | bytes 933896 | tf_op jit(solution)/shard_map/ppermute | solution.py:349
  86.9 2.7 %collective-permute-start.7 = (s16[4,304,128]{2,1,0:T(8,128)(2,1)S(1)}, s16[4,304,128]{2,1,0:T(8,128)(2,1)S(1)}, u32[]{:S(2)}, u32[]{:S(2)}) collective-permute-start(s16[4,304,128]{2,1,0:T(8,128)(2,1)S(1)} %collective-permute-done.4.refs_1_), channel_id=1, source_target_pairs={{0,4},{4,0},{8,12},{12,8},{16,20},{20,16},{24,28},{28,24},{32,36},... | collective-permute-start | bytes 933896 | tf_op jit(solution)/shard_map/ppermute | solution.py:352
